TPU v7x, 256 devices: a whole 4x4x8 slice. The times are simulated.
256 devices in a mesh: gx: 16 (over y_hi, x, core), gy: 16 (over z, y_lo).
Axes of the slice: x: 4, y: 4 (y_hi: 2, y_lo: 2; y = y_hi * 2 + y_lo), z: 8, core: 2. Of those that a mesh axis runs over, the one named last changes fastest.
Arguments:
- state: float32 [16, 16, 256, 8, 128], P('gx', 'gy'), may hold values from -4 to 6, as said below
- heavy_flag: int32 [16, 16], P('gx', 'gy'), may hold values from 0 to 1, as said below
- order: int32 [16, 16, 256], P('gx', 'gy'), may hold values from 0 to 255, as said below
- send: int32 [16, 16, 64], P('gx', 'gy'), may hold values from 0 to 255, as said below
- nbr: int32 [16, 16, 256, 8], P('gx', 'gy'), may hold values from -1 to 575, as said below
Outputs:
- rates: float32 [16, 16, 256, 4, 128], P('gx', 'gy')
Inputs may be any that keep to these rules, and one draw needn't show every extreme that they name: `state`: components in order: position x, y, z in 0 to 6, velocity u, v, w in -4 to 4, density in 0.95 to 1.05, mass in 0.02 to 0.08. `heavy_flag`: the devices at gx index g and g + 8 of one gy column are a matched pair, and exactly one of the two has flag 1. `order`: A permutation of the device's 256 slots. On a light device the first 128 entries are its live tiles. `send`: distinct slots of the device; on a light device all among its live tiles. `nbr`: distinct entries per tile, each an index into the device's extended list or -1; the -1 entries stand at the end, at most 2 of them. No entry names a grid offset outside the grid, and none names a tile of the device itself that is not live.
All inputs are finite; a program needn't handle non-finite values.
Results may differ from a plain program's by a relative error of at most 0.0003.
Values sent between devices are 32-bit elements; how exact they have to be, the bound alone decides.
A program may use at most 64 MiB of HBM per device.

v0:
```python
import math

import jax
import jax.numpy as jnp
from jax import lax
from jax.sharding import PartitionSpec as P

HS_CORNER = 16


KERNEL_NORM = 21.0 / (16.0 * math.pi)
STIFFNESS = 5.0
SOUND_SPEED = math.sqrt(35.0)
VISCOSITY = 0.1
SOFTENING = 0.01


def padded(block, sides, width):
    for axis, dim in sides:
        count = lax.axis_size(axis)
        forward = [(i, i + 1) for i in range(count - 1)]
        backward = [(target, source) for source, target in forward]
        low = lax.ppermute(
            lax.slice_in_dim(block, block.shape[dim] - width, None, axis=dim), axis, forward
        )
        high = lax.ppermute(lax.slice_in_dim(block, 0, width, axis=dim), axis, backward)
        block = jnp.concatenate([low, block, high], axis=dim)
    return block


def pair_sums(own_tiles, other_tiles):
    sep_x = own_tiles[..., 0, :, None] - other_tiles[..., 0, None, :]
    sep_y = own_tiles[..., 1, :, None] - other_tiles[..., 1, None, :]
    sep_z = own_tiles[..., 2, :, None] - other_tiles[..., 2, None, :]
    rel_u = own_tiles[..., 3, :, None] - other_tiles[..., 3, None, :]
    rel_v = own_tiles[..., 4, :, None] - other_tiles[..., 4, None, :]
    rel_w = own_tiles[..., 5, :, None] - other_tiles[..., 5, None, :]
    rho_i = own_tiles[..., 6, :, None]
    rho_j = other_tiles[..., 6, None, :]
    mass_j = other_tiles[..., 7, None, :]
    dist_sq = sep_x * sep_x + sep_y * sep_y + sep_z * sep_z
    reach_left = jnp.maximum(1.0 - 0.5 * jnp.sqrt(dist_sq), 0.0)
    kernel_slope = -5.0 * KERNEL_NORM * reach_left * reach_left * reach_left
    press_i = STIFFNESS * (rho_i**7 - 1.0) / (rho_i * rho_i)
    press_j = STIFFNESS * (rho_j**7 - 1.0) / (rho_j * rho_j)
    closing = rel_u * sep_x + rel_v * sep_y + rel_w * sep_z
    viscous = (
        -VISCOSITY
        * SOUND_SPEED
        * 2.0
        * jnp.minimum(closing, 0.0)
        / ((dist_sq + SOFTENING) * (rho_i + rho_j))
    )
    push_term = mass_j * (press_i + press_j + viscous) * kernel_slope
    accel_x = -jnp.sum(push_term * sep_x, axis=-1)
    accel_y = -jnp.sum(push_term * sep_y, axis=-1)
    accel_z = -jnp.sum(push_term * sep_z, axis=-1)
    density_rate = jnp.sum(mass_j * kernel_slope * closing, axis=-1)
    return jnp.stack([accel_x, accel_y, accel_z, density_rate], axis=-2)


def tile_sums(own_tiles, columns, fetch):

    def accumulate(running, column):
        return (running + pair_sums(own_tiles, fetch(column)), None)

    start = jnp.zeros((own_tiles.shape[0], 4, own_tiles.shape[2]), jnp.float32)
    return lax.scan(accumulate, start, columns)[0]


def shards(state, heavy_flag, order, send, nbr):
    own_tiles = state[0, 0]
    slot_count = own_tiles.shape[0]
    face_rows = send.shape[2]
    corner_rows = HS_CORNER
    outgoing = jnp.take(own_tiles, send[0, 0], axis=0)[None, None]
    beside_all = padded(outgoing, (("gx", 0), ("gy", 1)), 1)
    pieces = [
        beside_all[0, 0, :corner_rows],
        beside_all[0, 1],
        beside_all[0, 2, :corner_rows],
        beside_all[1, 0],
        beside_all[1, 2],
        beside_all[2, 0, :corner_rows],
        beside_all[2, 1],
        beside_all[2, 2, :corner_rows],
    ]
    blank_tile = jnp.zeros(own_tiles.shape[1:], jnp.float32).at[6].set(1.0)
    extended = jnp.concatenate([own_tiles] + pieces + [blank_tile[None]], axis=0)
    extent = slot_count + 4 * face_rows + 4 * corner_rows
    tile_lists = jnp.where(nbr[0, 0] < 0, extent, nbr[0, 0])
    is_heavy = heavy_flag[0, 0] == 1
    sequence = order[0, 0]
    light_live = slot_count // 2

    def fetch_extended(column):
        return jnp.take(extended, column, axis=0)

    tile_rates = tile_sums(own_tiles, tile_lists.T, fetch_extended)
    slot_ids = jnp.arange(slot_count, dtype=jnp.int32)
    member = jnp.any(sequence[:light_live, None] == slot_ids[None, :], axis=0)
    live_mask = is_heavy | member
    result = jnp.where(live_mask[:, None, None], tile_rates, 0.0)
    return result[None, None]


def solution(mesh):
    in_specs = (
        P("gx", "gy", None, None, None),
        P("gx", "gy"),
        P("gx", "gy", None),
        P("gx", "gy", None),
        P("gx", "gy", None, None),
    )
    out_specs = P("gx", "gy", None, None, None)
    return jax.shard_map(shards, mesh=mesh, in_specs=in_specs, out_specs=out_specs, check_vma=False)
```

profile of v0, /device:TPU:32, one launch (start us, length us, event | category | flops | bytes accessed | tf_op | source)
XLA Modules:
  0.0 537.3 jit_solution(4429848550775050850)
XLA Ops:
  1.4 1.8 gather_fusion.1
  3.4 1.8 collective-permute-start
  7.8 2.0 collective-permute-done.1
  10.8 3.5 collective-permute-start.2
  15.2 3.3 collective-permute-start.3
  18.8 26.7 %collective-permute-done.2 = f32[3,1,64,8,128]{4,3,2,1,0:T(8,128)} collective-permute-done((f32[3,1,64,8,128]{4,3,2,1,0:T(8,128)}, f32[3,1,64,8,128]{4,3,2,1,0:T(8,128)}, u32[]{:S(2)}, u32[]{:S(2)}) %collective-permute-start.2) | collective-permute-done | bytes 786464 | tf_op jit(solution)/shard_map/ppermute | solution.py:23
  46.3 4.7 collective-permute-done.3
  57.0 479.1 %while.15 = (s32[]{:T(128)}, f32[256,4,128]{2,0,1:T(8,128)S(1)}, s32[8,256]{1,0:T(8,128)S(1)}, f32[577,8,128]{2,1,0:T(8,128)}, f32[256,128,1]{1,0,2:T(8,128)S(1)...) while((s32[]{:T(128)}, f32[256,4,128]{2,0,1:T(8,128)S(1)}, ...), condition=%wide.region_6.7_spmd.clone, body=%wide.region_1.6_spmd.clone.sunk | while | flops 173182208 | bytes 13773419 | solution.py:68
  57.0 2.4 gather_fusion
  59.9 56.7 %fusion.30 = (f32[256,128]{1,0:T(8,128)S(1)}, f32[256,128]{1,0:T(8,128)S(1)}, f32[256,128]{1,0:T(8,128)S(1)}, f32[256,128]{1,0:T(8,128)S(1)}) fusion(f32[256,128]{1,0:T(8,128)S(1)} %get-tuple-element.295, f32[256,128]{1,0:T(8,128)S(1)} %get-tuple-element.296, f32[256,128]{1,0:T(8,128)S(1)} %get-tuple-element.297, ...), kind=kLoop, calls=%fused_computation.16.clone.1 | loop fusion | flops 171835392 | bytes 2752512 | tf_op jit(solution)/shard_map/while/body/eval_jaxpr/reduce_sum | solution.py:55
  116.9 2.4 gather_fusion
  119.8 56.7 %fusion.30 = (f32[256,128]{1,0:T(8,128)S(1)}, f32[256,128]{1,0:T(8,128)S(1)}, f32[256,128]{1,0:T(8,128)S(1)}, f32[256,128]{1,0:T(8,128)S(1)}) fusion(f32[256,128]{1,0:T(8,128)S(1)} %get-tuple-element.295, f32[256,128]{1,0:T(8,128)S(1)} %get-tuple-element.296, f32[256,128]{1,0:T(8,128)S(1)} %get-tuple-element.297, ...), kind=kLoop, calls=%fused_computation.16.clone.1 | loop fusion | flops 171835392 | bytes 2752512 | tf_op jit(solution)/shard_map/while/body/eval_jaxpr/reduce_sum | solution.py:55
  176.8 2.4 gather_fusion
  179.7 56.7 %fusion.30 = (f32[256,128]{1,0:T(8,128)S(1)}, f32[256,128]{1,0:T(8,128)S(1)}, f32[256,128]{1,0:T(8,128)S(1)}, f32[256,128]{1,0:T(8,128)S(1)}) fusion(f32[256,128]{1,0:T(8,128)S(1)} %get-tuple-element.295, f32[256,128]{1,0:T(8,128)S(1)} %get-tuple-element.296, f32[256,128]{1,0:T(8,128)S(1)} %get-tuple-element.297, ...), kind=kLoop, calls=%fused_computation.16.clone.1 | loop fusion | flops 171835392 | bytes 2752512 | tf_op jit(solution)/shard_map/while/body/eval_jaxpr/reduce_sum | solution.py:55
  236.7 2.4 gather_fusion
  239.6 56.7 %fusion.30 = (f32[256,128]{1,0:T(8,128)S(1)}, f32[256,128]{1,0:T(8,128)S(1)}, f32[256,128]{1,0:T(8,128)S(1)}, f32[256,128]{1,0:T(8,128)S(1)}) fusion(f32[256,128]{1,0:T(8,128)S(1)} %get-tuple-element.295, f32[256,128]{1,0:T(8,128)S(1)} %get-tuple-element.296, f32[256,128]{1,0:T(8,128)S(1)} %get-tuple-element.297, ...), kind=kLoop, calls=%fused_computation.16.clone.1 | loop fusion | flops 171835392 | bytes 2752512 | tf_op jit(solution)/shard_map/while/body/eval_jaxpr/reduce_sum | solution.py:55
  296.6 2.4 gather_fusion
  299.5 56.7 %fusion.30 = (f32[256,128]{1,0:T(8,128)S(1)}, f32[256,128]{1,0:T(8,128)S(1)}, f32[256,128]{1,0:T(8,128)S(1)}, f32[256,128]{1,0:T(8,128)S(1)}) fusion(f32[256,128]{1,0:T(8,128)S(1)} %get-tuple-element.295, f32[256,128]{1,0:T(8,128)S(1)} %get-tuple-element.296, f32[256,128]{1,0:T(8,128)S(1)} %get-tuple-element.297, ...), kind=kLoop, calls=%fused_computation.16.clone.1 | loop fusion | flops 171835392 | bytes 2752512 | tf_op jit(solution)/shard_map/while/body/eval_jaxpr/reduce_sum | solution.py:55
  356.4 2.4 gather_fusion
  359.4 56.7 %fusion.30 = (f32[256,128]{1,0:T(8,128)S(1)}, f32[256,128]{1,0:T(8,128)S(1)}, f32[256,128]{1,0:T(8,128)S(1)}, f32[256,128]{1,0:T(8,128)S(1)}) fusion(f32[256,128]{1,0:T(8,128)S(1)} %get-tuple-element.295, f32[256,128]{1,0:T(8,128)S(1)} %get-tuple-element.296, f32[256,128]{1,0:T(8,128)S(1)} %get-tuple-element.297, ...), kind=kLoop, calls=%fused_computation.16.clone.1 | loop fusion | flops 171835392 | bytes 2752512 | tf_op jit(solution)/shard_map/while/body/eval_jaxpr/reduce_sum | solution.py:55
  416.3 2.4 gather_fusion
  419.3 56.7 %fusion.30 = (f32[256,128]{1,0:T(8,128)S(1)}, f32[256,128]{1,0:T(8,128)S(1)}, f32[256,128]{1,0:T(8,128)S(1)}, f32[256,128]{1,0:T(8,128)S(1)}) fusion(f32[256,128]{1,0:T(8,128)S(1)} %get-tuple-element.295, f32[256,128]{1,0:T(8,128)S(1)} %get-tuple-element.296, f32[256,128]{1,0:T(8,128)S(1)} %get-tuple-element.297, ...), kind=kLoop, calls=%fused_computation.16.clone.1 | loop fusion | flops 171835392 | bytes 2752512 | tf_op jit(solution)/shard_map/while/body/eval_jaxpr/reduce_sum | solution.py:55
  476.2 2.4 gather_fusion
  479.2 56.7 %fusion.30 = (f32[256,128]{1,0:T(8,128)S(1)}, f32[256,128]{1,0:T(8,128)S(1)}, f32[256,128]{1,0:T(8,128)S(1)}, f32[256,128]{1,0:T(8,128)S(1)}) fusion(f32[256,128]{1,0:T(8,128)S(1)} %get-tuple-element.295, f32[256,128]{1,0:T(8,128)S(1)} %get-tuple-element.296, f32[256,128]{1,0:T(8,128)S(1)} %get-tuple-element.297, ...), kind=kLoop, calls=%fused_computation.16.clone.1 | loop fusion | flops 171835392 | bytes 2752512 | tf_op jit(solution)/shard_map/while/body/eval_jaxpr/reduce_sum | solution.py:55
  (112 shorter events, 18.8 us)
Async XLA Ops:
  0.0 14.4 %copy-start.1 = (f32[1,1,256,8,128]{4,3,2,1,0:T(8,128)S(1)}, f32[1,1,256,8,128]{4,3,2,1,0:T(8,128)}, u32[]{:S(2)}) copy-start(f32[1,1,256,8,128]{4,3,2,1,0:T(8,128)} %param.9) | copy-start | bytes 3145732
  3.4 4.4 collective-permute-start
  5.2 4.7 collective-permute-start.1
  10.8 34.7 %collective-permute-start.2 = (f32[3,1,64,8,128]{4,3,2,1,0:T(8,128)}, f32[3,1,64,8,128]{4,3,2,1,0:T(8,128)}, u32[]{:S(2)}, u32[]{:S(2)}) collective-permute-start(f32[3,1,64,8,128]{4,3,2,1,0:T(8,128)} %pad_maximum_fusion), channel_id=1, source_target_pairs={{0,1},{1,2},{2,3},{3,4},{4,5},{5,6},{6,7},{7,8},{8,9},{9,10},{10,1... | collective-permute-start | bytes 2359304 | tf_op jit(solution)/shard_map/ppermute | solution.py:23
  15.2 35.9 %collective-permute-start.3 = (f32[3,1,64,8,128]{4,3,2,1,0:T(8,128)}, f32[3,1,64,8,128]{4,3,2,1,0:T(8,128)}, u32[]{:S(2)}, u32[]{:S(2)}) collective-permute-start(f32[3,1,64,8,128]{4,3,2,1,0:T(8,128)} %pad_maximum_fusion), channel_id=1, source_target_pairs={{1,0},{2,1},{3,2},{4,3},{5,4},{6,5},{7,6},{8,7},{9,8},{10,9},{11,1... | collective-permute-start | bytes 2359304 | tf_op jit(solution)/shard_map/ppermute | solution.py:26
  18.7 36.9 %copy-start.2 = (f32[1,8,128]{2,1,0:T(8,128)S(1)}, f32[1,8,128]{2,1,0:T(8,128)}, u32[]{:S(2)}) copy-start(f32[1,8,128]{2,1,0:T(8,128)} %constant.155.clone.1) | copy-start | bytes 12292
  55.6 1.4 copy-start
where the time goes:
time: 544 us; the launch traced here: 537 us
  other arithmetic  463 us (85%)
  waiting for transfers between devices  33.4 us (6%)
  local copies, waits for them, and re-layouts  29.5 us (5%)
  starting transfers between devices  9.78 us (2%)
    reduce_sum x8, other arithmetic, pair_sums(): accel_x = -jnp.sum(push_term * sep_x, axis=-1)  454 us
    ppermute x2, waiting for transfers between devices, padded(): lax.ppermute(lax.slice_in_dim(block, block.shape[dim] - width, None, axis...  26.7 us
    gather x8, local copies, waits for them, and re-layouts, fetch_extended(): return jnp.take(extended, column, axis=0)  19.4 us
  transfers between devices with their start and end apart: 4, of which 3 were waited for; matrix products, arithmetic and copies ran while one was open for 1% of the time, Pallas kernels for 0%

commit v1 on v0

v1 whole, which is shorter than its diff:
```python
import math

import jax
import jax.numpy as jnp
from jax import lax
from jax.experimental import pallas as pl
from jax.experimental.pallas import tpu as pltpu
from jax.sharding import PartitionSpec as P

TPD = 256
NEIGHBOURS = 8
LIGHT = 128
HS_FACE = 64
HS_CORNER = 16
EXT = 576
OFFSETS = ((-1, -1), (-1, 0), (-1, 1), (0, -1), (0, 1), (1, -1), (1, 0), (1, 1))

SLOPE = -5.0 * 21.0 / (16.0 * math.pi)
ALPHA = 0.1 * math.sqrt(35.0) * 2.0
GAMMA = 2.0 / ALPHA
SOFT = 0.01 / 4.0
OWN_PART = (0, 0, 0, 1, 1, 2)
OTHER_PART = (0, 1, 2, 0, 1, 0)
BLOCKS = ((0, 0), (0, 1), (1, 0), (2, 0), (2, 1), (3, 0), (3, 1))
bf16, f32 = jnp.bfloat16, jnp.float32


def split3(v):
    hi = v.astype(bf16).astype(f32)
    rest = v - hi
    mid = rest.astype(bf16).astype(f32)
    return hi, mid, rest - mid


def fields(src, first):
    flat = src.reshape(src.shape[0] * 8, 128)

    def row(c):
        return flat[pl.ds(first * 8 + c, 8, stride=8), :]

    x, y, z = ((row(c) - 3.0) * 0.5 for c in range(3))
    u, v, w, rho, m = (row(c) for c in range(3, 8))
    r2 = rho * rho
    r4 = r2 * r2
    p = 5.0 * (r4 * r2 * rho - 1.0) / r2
    return x, y, z, u, v, w, rho, m, p, x * x + y * y + z * z, u * x + v * y + w * z


def other_rows(src, first):
    x, y, z, u, v, w, rho, m, p, xx, vx = fields(src, first)
    one = jnp.ones_like(x)
    gr = GAMMA * rho
    g2 = 2.0 * GAMMA
    return {
        (0, 3): 2.0 * x, (0, 4): 2.0 * y, (0, 5): 2.0 * z, (0, 7): xx, (0, 8): one,
        (1, 0): m * x, (1, 1): m * y, (1, 2): m * z, (1, 3): m * u, (1, 4): m * v, (1, 5): m * w,
        (1, 6): m, (1, 7): m * vx,
        (2, 3): 2.0 * gr * x, (2, 4): 2.0 * gr * y, (2, 5): 2.0 * gr * z, (2, 7): gr * (xx + SOFT), (2, 8): gr,
        (2, 9): g2 * x, (2, 10): g2 * y, (2, 11): g2 * z, (2, 12): GAMMA * one, (2, 13): GAMMA * xx,
        (3, 7): m * p, (3, 14): m,
    }


def own_rows(src, first):
    x, y, z, u, v, w, rho, m, p, xx, vx = fields(src, first)
    return (
        -u, -v, -w, -x, -y, -z, vx, jnp.ones_like(x),
        xx, -rho * x, -rho * y, -rho * z, rho * (xx + SOFT), rho, p,
    )


def other_tables(src, first, dest, stage, table, place):
    for (q, r), value in other_rows(src, first).items():
        b = BLOCKS.index((q, r // 8))
        for part, v in enumerate(split3(value)):
            stage[pl.ds(((b * 3 + part) * 8 + r % 8) * 8, 8), :] = v
    zero = jnp.zeros((8, 128), f32)
    for i in range(8):
        for part in range(3):
            for q in range(4):
                halves = [
                    stage[pl.ds((BLOCKS.index((q, h)) * 3 + part) * 64 + i, 8, stride=8), :]
                    if (q, h) in BLOCKS else zero
                    for h in range(2)
                ]
                at = part * 64 + q * 16
                table[dest + i, at:at + 16, :] = jnp.concatenate(halves, 0).astype(bf16)
        place[dest + i] = (src[first + i] - 3.0) * 0.5


def own_tables(src, first, stage, table):
    for r, value in enumerate(own_rows(src, first)):
        for part, v in enumerate(split3(value)):
            stage[pl.ds((((r // 8) * 3 + part) * 8 + r % 8) * 8, 8), :] = v
    for i in range(8):
        for part in range(3):
            for h in range(2):
                at = part * 16 + h * 8
                table[first + i, at:at + 8, :] = stage[pl.ds((h * 3 + part) * 64 + i, 8, stride=8), :]


def own_side(rows):
    parts = [rows[i * 16:(i + 1) * 16] for i in range(3)]
    return jnp.concatenate([parts[p] for p in OWN_PART], 0).T.astype(bf16)


def other_side(table, e):
    return jnp.concatenate(
        [
            jnp.concatenate([table[e, pl.ds(p * 64 + q * 16, 16), :] for p in OTHER_PART], 0)
            for q in range(4)
        ],
        1,
    )


def pair(own, other):
    g = jnp.dot(own, other, preferred_element_type=f32)
    h, c, d, a = (g[:, i * 128:(i + 1) * 128] for i in range(4))
    h = jnp.maximum(h, 1e-30)
    reach = jnp.maximum(1.0 - h * lax.rsqrt(h), 0.0)
    cube = reach * reach * reach
    push = (a - jnp.minimum(c, 0.0) * pl.reciprocal(d, approx=True)) * cube
    return push, cube * c


def tile_sums(own, entries, table, place):
    sums = None
    for e in entries:
        push, rate = pair(own, other_side(table, e))
        new = [push * place[e, 0:1], push * place[e, 1:2], push * place[e, 2:3], push, rate]
        sums = new if sums is None else [a + b for a, b in zip(sums, new)]
    return sums


def finish(acc, t, place, out):
    totals = [jnp.sum(acc[q].T, 0, keepdims=True) for q in range(5)]
    out[t, 0:3] = (-2.0 * SLOPE) * (place[t][:3] * totals[3] - jnp.concatenate(totals[:3], 0))
    out[t, 3:4] = (2.0 * SLOPE) * totals[4]


def rates_kernel(heavy, order, nbr, own, *rest):
    pieces, (out, stage, table, own_stage, own_table, acc, place, lists, counts) = rest[:8], rest[8:]
    stage[...] = jnp.zeros_like(stage)
    own_stage[...] = jnp.zeros_like(own_stage)
    live = LIGHT + (TPD - LIGHT) * heavy[0]

    base = 0
    for src in (own, *pieces):
        def build(b, _, src=src, base=base):
            other_tables(src, b * 8, base + b * 8, stage, table, place)
            return 0

        lax.fori_loop(0, src.shape[0] // 8, build, 0)
        base += src.shape[0]

    def build_own(b, _):
        own_tables(own, b * 8, own_stage, own_table)
        return 0

    lax.fori_loop(0, TPD // 8, build_own, 0)

    for g in range(3):
        counts[g] = 0

    def sort(s, _):
        t = order[s]
        g = jnp.where(nbr[t * NEIGHBOURS + 6] >= 0, 1, 0) + jnp.where(nbr[t * NEIGHBOURS + 7] >= 0, 1, 0)
        n = counts[g]
        lists[g * TPD + n] = t
        counts[g] = n + 1
        return 0

    lax.fori_loop(0, live, sort, 0)

    def clear(s, _):
        out[order[s]] = jnp.zeros((4, 128), f32)
        return 0

    lax.fori_loop(live, TPD, clear, 0)

    for g in range(3):
        n = counts[g]

        def tile(s, mine, g=g, n=n):
            t = lists[g * TPD + s]
            finish(acc, lists[g * TPD + jnp.maximum(s - 1, 0)], place, out)
            following = own_side(own_table[lists[g * TPD + jnp.minimum(s + 1, n - 1)]])
            entries = [nbr[t * NEIGHBOURS + k] for k in range(6 + g)]
            for q, value in enumerate(tile_sums(mine, entries, table, place)):
                acc[q] = value
            return following

        @pl.when(n > 0)
        def _(tile=tile, g=g, n=n):
            lax.fori_loop(0, n, tile, own_side(own_table[lists[g * TPD]]))
            finish(acc, lists[g * TPD + n - 1], place, out)


def shards(state, heavy_flag, order, send, nbr):
    own = state[0, 0]
    outgoing = jnp.take(own, send[0, 0], axis=0)
    n_gx, n_gy = lax.axis_size("gx"), lax.axis_size("gy")
    pieces = []
    for p, q in OFFSETS:
        count = HS_CORNER if p and q else HS_FACE
        perm = [
            ((a + p) * n_gy + b + q, a * n_gy + b)
            for a in range(n_gx) for b in range(n_gy)
            if 0 <= a + p < n_gx and 0 <= b + q < n_gy
        ]
        pieces.append(lax.ppermute(outgoing[:count], ("gx", "gy"), perm))
    smem = pl.BlockSpec(memory_space=pltpu.SMEM)
    vmem = pl.BlockSpec(memory_space=pltpu.VMEM)
    rates = pl.pallas_call(
        rates_kernel,
        out_shape=jax.ShapeDtypeStruct((TPD, 4, 128), f32),
        in_specs=[smem] * 3 + [vmem] * 9,
        out_specs=vmem,
        scratch_shapes=[
            pltpu.VMEM((7 * 3 * 64, 128), f32),
            pltpu.VMEM((EXT, 192, 128), bf16),
            pltpu.VMEM((2 * 3 * 64, 128), f32),
            pltpu.VMEM((TPD, 48, 128), f32),
            pltpu.VMEM((5, 128, 128), f32),
            pltpu.VMEM((EXT, 8, 128), f32),
            pltpu.SMEM((3 * TPD,), jnp.int32),
            pltpu.SMEM((3,), jnp.int32),
        ],
        compiler_params=pltpu.CompilerParams(vmem_limit_bytes=56 * 2**20),
    )(heavy_flag[0], order[0, 0], nbr[0, 0].reshape(-1), own, *pieces)
    return rates[None, None]


def solution(mesh):
    in_specs = (
        P("gx", "gy", None, None, None),
        P("gx", "gy"),
        P("gx", "gy", None),
        P("gx", "gy", None),
        P("gx", "gy", None, None),
    )
    out_specs = P("gx", "gy", None, None, None)
    return jax.shard_map(shards, mesh=mesh, in_specs=in_specs, out_specs=out_specs, check_vma=False)
```

time: 544 us -> 203 us (0.37)
  the two profiles are of different devices: /device:TPU:32 before, /device:TPU:24 now
where the time goes in v1:
time: 203 us; the launch traced here: 202 us
  Pallas kernels  154 us (76%)
  starting transfers between devices  27.3 us (13%)
  waiting for transfers between devices  15.5 us (8%)
  local copies, waits for them, and re-layouts  3.61 us (2%)
    pallas_call x1, Pallas kernels, shards(): pl.pallas_call(rates_kernel, out_shape=jax.ShapeDtypeStruct((TPD, 4, 128)...  154 us
    ppermute x8, starting transfers between devices, shards(): pieces.append(lax.ppermute(outgoing[:count], ('gx', 'gy'), perm))  27.3 us
    ppermute x8, waiting for transfers between devices, shards(): pieces.append(lax.ppermute(outgoing[:count], ('gx', 'gy'), perm))  15.5 us
  transfers between devices with their start and end apart: 8, of which 3 were waited for; matrix products, arithmetic and copies ran while one was open for 0% of the time, Pallas kernels for 0%

profile of v1, /device:TPU:24, one launch (start us, length us, event | category | flops | bytes accessed | tf_op | source)
XLA Modules:
  0.0 202.2 jit_solution(1061139186780523018)
XLA Ops:
  0.0 0.7 fusion
  0.8 1.8 gather_fusion
  2.6 0.1 broadcast_select_fusion
  2.7 0.0 copy-start.8
  2.8 3.8 %collective-permute-start.7 = (f32[16,8,128]{2,1,0:T(8,128)S(1)}, f32[16,8,128]{2,1,0:T(8,128)S(1)}, u32[]{:S(2)}, u32[]{:S(2)}) collective-permute-start(f32[16,8,128]{2,1,0:T(8,128)S(1)} %slice.9), channel_id=1, source_target_pairs={{17,0},{18,1},{19,2},{20,3},{21,4},{22,5},{23,6},{24,7},{25,8},{26... | collective-permute-start | bytes 196616 | tf_op jit(solution)/shard_map/ppermute | solution.py:212
  6.5 3.7 %collective-permute-start.6 = (f32[64,8,128]{2,1,0:T(8,128)S(1)}, f32[64,8,128]{2,1,0:T(8,128)S(1)}, u32[]{:S(2)}, u32[]{:S(2)}) collective-permute-start(f32[64,8,128]{2,1,0:T(8,128)S(1)} %broadcast_select_fusion), channel_id=1, source_target_pairs={{16,0},{17,1},{18,2},{19,3},{20,4},{21,5},{22,6},{23,7},{24,8},{25... | collective-permute-start | bytes 786440 | tf_op jit(solution)/shard_map/ppermute | solution.py:212
  10.2 1.9 collective-permute-start.4
  12.1 4.8 %collective-permute-start.3 = (f32[64,8,128]{2,1,0:T(8,128)S(1)}, f32[64,8,128]{2,1,0:T(8,128)S(1)}, u32[]{:S(2)}, u32[]{:S(2)}) collective-permute-start(f32[64,8,128]{2,1,0:T(8,128)S(1)} %broadcast_select_fusion), channel_id=1, source_target_pairs={{0,1},{1,2},{2,3},{3,4},{4,5},{5,6},{6,7},{7,8},{8,9},{9,10},{10,1... | collective-permute-start | bytes 786440 | tf_op jit(solution)/shard_map/ppermute | solution.py:212
  16.9 1.9 collective-permute-start.1
  18.9 0.0 collective-permute-done.7.rest_7_
  18.9 7.4 %collective-permute-start.5 = (f32[16,8,128]{2,1,0:T(8,128)S(1)}, f32[16,8,128]{2,1,0:T(8,128)S(1)}, u32[]{:S(2)}, u32[]{:S(2)}) collective-permute-start(f32[16,8,128]{2,1,0:T(8,128)S(1)} %slice.9), channel_id=1, source_target_pairs={{16,1},{17,2},{18,3},{19,4},{20,5},{21,6},{22,7},{23,8},{24,9},{25... | collective-permute-start | bytes 196616 | tf_op jit(solution)/shard_map/ppermute | solution.py:212
  26.3 1.9 collective-permute-done.5.rest_5_
  28.2 1.9 collective-permute-start.2
  30.1 8.2 %collective-permute-done.2.rest_2_ = f32[16,8,128]{2,1,0:T(8,128)S(1)} collective-permute-done((f32[16,8,128]{2,1,0:T(8,128)S(1)}, f32[16,8,128]{2,1,0:T(8,128)S(1)}, u32[]{:S(2)}, u32[]{:S(2)}) %collective-permute-start.2) | collective-permute-done | bytes 65568 | tf_op jit(solution)/shard_map/ppermute | solution.py:212
  38.2 1.9 collective-permute-start
  40.8 0.1 copy.6
  41.0 0.7 reshape_squeeze.3.nbr
  41.7 5.5 %collective-permute-done.rest_0_ = f32[16,8,128]{2,1,0:T(8,128)S(1)} collective-permute-done((f32[16,8,128]{2,1,0:T(8,128)S(1)}, f32[16,8,128]{2,1,0:T(8,128)S(1)}, u32[]{:S(2)}, u32[]{:S(2)}) %collective-permute-start) | collective-permute-done | bytes 65568 | tf_op jit(solution)/shard_map/ppermute | solution.py:212
  47.2 0.5 copy-done.7
  47.7 0.1 copy-done
  47.9 0.1 copy-done.1
  47.9 0.1 copy-done.2
  48.0 0.1 copy-done.3
  48.1 154.1 %shard_map.55 = f32[256,4,128]{2,1,0:T(4,128)} custom-call(s32[1]{0:T(128)} %bitcast.12.heavy, s32[256]{0:T(256)} %bitcast.15, s32[2048]{0:T(1024)} %reshape_squeeze.3.nbr, f32[256,8,128]{2,1,0:T(8,128)} %bitcast.14, f32[16,8,128]{2,1,0:T(8,128)} %copy-done.7, f32[64,8,128]{2,1,0:T(8,128)} %copy-done.3, f32[16,8,128]{2,1,0:T(8,128)} %copy-done.6, ...), custom_call_target="tpu_custom_call" | custom-call | tf_op jit(solution)/shard_map/pallas_call | solution.py:215
  (21 shorter events, 0.1 us)
Async XLA Ops:
  0.0 0.7 copy-start.9
  2.7 38.1 %copy-start.8 = (s32[1,1,256,8]{2,3,1,0:T(8,128)S(1)}, s32[1,1,256,8]{2,3,1,0:T(8,128)}, u32[]{:S(2)}) copy-start(s32[1,1,256,8]{2,3,1,0:T(8,128)} %param.9) | copy-start | bytes 24580
  2.8 16.1 %collective-permute-start.7 = (f32[16,8,128]{2,1,0:T(8,128)S(1)}, f32[16,8,128]{2,1,0:T(8,128)S(1)}, u32[]{:S(2)}, u32[]{:S(2)}) collective-permute-start(f32[16,8,128]{2,1,0:T(8,128)S(1)} %slice.9), channel_id=1, source_target_pairs={{17,0},{18,1},{19,2},{20,3},{21,4},{22,5},{23,6},{24,7},{25,8},{26... | collective-permute-start | bytes 196616 | tf_op jit(solution)/shard_map/ppermute | solution.py:212
  6.5 40.6 %collective-permute-start.6 = (f32[64,8,128]{2,1,0:T(8,128)S(1)}, f32[64,8,128]{2,1,0:T(8,128)S(1)}, u32[]{:S(2)}, u32[]{:S(2)}) collective-permute-start(f32[64,8,128]{2,1,0:T(8,128)S(1)} %broadcast_select_fusion), channel_id=1, source_target_pairs={{16,0},{17,1},{18,2},{19,3},{20,4},{21,5},{22,6},{23,7},{24,8},{25... | collective-permute-start | bytes 786440 | tf_op jit(solution)/shard_map/ppermute | solution.py:212
  10.2 36.9 %collective-permute-start.4 = (f32[64,8,128]{2,1,0:T(8,128)S(1)}, f32[64,8,128]{2,1,0:T(8,128)S(1)}, u32[]{:S(2)}, u32[]{:S(2)}) collective-permute-start(f32[64,8,128]{2,1,0:T(8,128)S(1)} %broadcast_select_fusion), channel_id=1, source_target_pairs={{1,0},{2,1},{3,2},{4,3},{5,4},{6,5},{7,6},{8,7},{9,8},{10,9},{11,1... | collective-permute-start | bytes 786440 | tf_op jit(solution)/shard_map/ppermute | solution.py:212
  12.1 35.0 %collective-permute-start.3 = (f32[64,8,128]{2,1,0:T(8,128)S(1)}, f32[64,8,128]{2,1,0:T(8,128)S(1)}, u32[]{:S(2)}, u32[]{:S(2)}) collective-permute-start(f32[64,8,128]{2,1,0:T(8,128)S(1)} %broadcast_select_fusion), channel_id=1, source_target_pairs={{0,1},{1,2},{2,3},{3,4},{4,5},{5,6},{6,7},{7,8},{8,9},{9,10},{10,1... | collective-permute-start | bytes 786440 | tf_op jit(solution)/shard_map/ppermute | solution.py:212
  16.9 30.2 %collective-permute-start.1 = (f32[64,8,128]{2,1,0:T(8,128)S(1)}, f32[64,8,128]{2,1,0:T(8,128)S(1)}, u32[]{:S(2)}, u32[]{:S(2)}) collective-permute-start(f32[64,8,128]{2,1,0:T(8,128)S(1)} %broadcast_select_fusion), channel_id=1, source_target_pairs={{0,16},{1,17},{2,18},{3,19},{4,20},{5,21},{6,22},{7,23},{8,24},{9,... | collective-permute-start | bytes 786440 | tf_op jit(solution)/shard_map/ppermute | solution.py:212
  18.9 22.0 %copy-start.4 = (f32[16,8,128]{2,1,0:T(8,128)}, f32[16,8,128]{2,1,0:T(8,128)S(1)}, u32[]{:S(2)}) copy-start(f32[16,8,128]{2,1,0:T(8,128)S(1)} %collective-permute-done.7.rest_7_) | copy-start | bytes 196612
  18.9 9.3 %collective-permute-start.5 = (f32[16,8,128]{2,1,0:T(8,128)S(1)}, f32[16,8,128]{2,1,0:T(8,128)S(1)}, u32[]{:S(2)}, u32[]{:S(2)}) collective-permute-start(f32[16,8,128]{2,1,0:T(8,128)S(1)} %slice.9), channel_id=1, source_target_pairs={{16,1},{17,2},{18,3},{19,4},{20,5},{21,6},{22,7},{23,8},{24,9},{25... | collective-permute-start | bytes 196616 | tf_op jit(solution)/shard_map/ppermute | solution.py:212
  28.2 12.8 %copy-start.5 = (f32[16,8,128]{2,1,0:T(8,128)}, f32[16,8,128]{2,1,0:T(8,128)S(1)}, u32[]{:S(2)}) copy-start(f32[16,8,128]{2,1,0:T(8,128)S(1)} %collective-permute-done.5.rest_5_) | copy-start | bytes 196612
  28.2 10.1 %collective-permute-start.2 = (f32[16,8,128]{2,1,0:T(8,128)S(1)}, f32[16,8,128]{2,1,0:T(8,128)S(1)}, u32[]{:S(2)}, u32[]{:S(2)}) collective-permute-start(f32[16,8,128]{2,1,0:T(8,128)S(1)} %slice.9), channel_id=1, source_target_pairs={{1,16},{2,17},{3,18},{4,19},{5,20},{6,21},{7,22},{8,23},{9,24},{10... | collective-permute-start | bytes 196616 | tf_op jit(solution)/shard_map/ppermute | solution.py:212
  38.2 9.0 %copy-start.6 = (f32[16,8,128]{2,1,0:T(8,128)}, f32[16,8,128]{2,1,0:T(8,128)S(1)}, u32[]{:S(2)}) copy-start(f32[16,8,128]{2,1,0:T(8,128)S(1)} %collective-permute-done.2.rest_2_) | copy-start | bytes 196612
  38.2 8.9 %collective-permute-start = (f32[16,8,128]{2,1,0:T(8,128)S(1)}, f32[16,8,128]{2,1,0:T(8,128)S(1)}, u32[]{:S(2)}, u32[]{:S(2)}) collective-permute-start(f32[16,8,128]{2,1,0:T(8,128)S(1)} %slice.9), channel_id=1, source_target_pairs={{0,17},{1,18},{2,19},{3,20},{4,21},{5,22},{6,23},{7,24},{8,25},{9,... | collective-permute-start | bytes 196616 | tf_op jit(solution)/shard_map/ppermute | solution.py:212
  47.1 0.6 copy-start.7
  47.1 0.7 copy-start
  47.1 0.8 copy-start.1
  47.2 0.9 copy-start.2
  47.2 0.9 copy-start.3

commit v2 on v1

--- a/solution.py
+++ b/solution.py
@@ -139,14 +139,13 @@
     out[t, 3:4] = (2.0 * SLOPE) * totals[4]
 
 
-def rates_kernel(heavy, order, nbr, own, *rest):
-    pieces, (out, stage, table, own_stage, own_table, acc, place, lists, counts) = rest[:8], rest[8:]
+def rates_kernel(heavy, order, nbr, own, halo, out, stage, table, own_stage, own_table, acc, place, lists, counts):
     stage[...] = jnp.zeros_like(stage)
     own_stage[...] = jnp.zeros_like(own_stage)
     live = LIGHT + (TPD - LIGHT) * heavy[0]
 
     base = 0
-    for src in (own, *pieces):
+    for src in (own, halo):
         def build(b, _, src=src, base=base):
             other_tables(src, b * 8, base + b * 8, stage, table, place)
             return 0
@@ -197,25 +196,103 @@
             finish(acc, lists[g * TPD + n - 1], place, out)
 
 
+def starts():
+    first, at = [], 0
+    for p, q in OFFSETS:
+        first.append(at)
+        at += HS_CORNER if p and q else HS_FACE
+    return first, at
+
+
+def exchange_kernel(n_gx, n_gy, send, own, halo, outgoing, send_sem, recv_sem):
+    a, b = lax.axis_index("gx"), lax.axis_index("gy")
+    first, _ = starts()
+
+    def beside(p, q):
+        inside = True
+        for at, step, count in ((a, p, n_gx), (b, q, n_gy)):
+            if step < 0:
+                inside = inside & (at > 0)
+            if step > 0:
+                inside = inside & (at < count - 1)
+        return inside
+
+    barrier = pltpu.get_barrier_semaphore()
+    for p, q in OFFSETS:
+        @pl.when(beside(p, q))
+        def _(p=p, q=q):
+            pl.semaphore_signal(barrier, inc=1, device_id=(a + p, b + q), device_id_type=pl.DeviceIdType.MESH)
+
+    def pick(s, _):
+        outgoing[s] = own[send[s]]
+        return 0
+
+    lax.fori_loop(0, HS_FACE, pick, 0)
+    rows = 1 + jnp.where(a > 0, 1, 0) + jnp.where(a < n_gx - 1, 1, 0)
+    cols = 1 + jnp.where(b > 0, 1, 0) + jnp.where(b < n_gy - 1, 1, 0)
+    pl.semaphore_wait(barrier, rows * cols - 1)
+
+    def copy(i, there):
+        p, q = OFFSETS[i]
+        count = HS_CORNER if p and q else HS_FACE
+        return pltpu.make_async_remote_copy(
+            src_ref=outgoing.at[pl.ds(0, count)],
+            dst_ref=halo.at[pl.ds(first[there], count)],
+            send_sem=send_sem.at[i],
+            recv_sem=recv_sem.at[there],
+            device_id=(a + p, b + q),
+            device_id_type=pl.DeviceIdType.MESH,
+        )
+
+    for i, (p, q) in enumerate(OFFSETS):
+        @pl.when(beside(p, q))
+        def _(i=i, p=p, q=q):
+            copy(i, OFFSETS.index((-p, -q))).start()
+
+    for i, (p, q) in enumerate(OFFSETS):
+        count = HS_CORNER if p and q else HS_FACE
+
+        @pl.when(jnp.logical_not(beside(p, q)))
+        def _(i=i, count=count):
+            halo[pl.ds(first[i], count)] = jnp.zeros((count, 8, 128), f32)
+
+    for i, (p, q) in enumerate(OFFSETS):
+        @pl.when(beside(p, q))
+        def _(i=i, p=p, q=q):
+            copy(i, OFFSETS.index((-p, -q))).wait_send()
+            copy(i, i).wait_recv()
+
+
+def exchange(own, send):
+    vmem = pl.BlockSpec(memory_space=pltpu.VMEM)
+    n_gx, n_gy = lax.axis_size("gx"), lax.axis_size("gy")
+
+    def kernel(*refs):
+        exchange_kernel(n_gx, n_gy, *refs)
+
+    return pl.pallas_call(
+        kernel,
+        out_shape=jax.ShapeDtypeStruct((starts()[1], 8, 128), f32),
+        in_specs=[pl.BlockSpec(memory_space=pltpu.SMEM), vmem],
+        out_specs=vmem,
+        scratch_shapes=[
+            pltpu.VMEM((HS_FACE, 8, 128), f32),
+            pltpu.SemaphoreType.DMA((8,)),
+            pltpu.SemaphoreType.DMA((8,)),
+        ],
+        compiler_params=pltpu.CompilerParams(collective_id=0, has_side_effects=True, vmem_limit_bytes=8 * 2**20),
+    )(send, own)
+
+
 def shards(state, heavy_flag, order, send, nbr):
     own = state[0, 0]
-    outgoing = jnp.take(own, send[0, 0], axis=0)
-    n_gx, n_gy = lax.axis_size("gx"), lax.axis_size("gy")
-    pieces = []
-    for p, q in OFFSETS:
-        count = HS_CORNER if p and q else HS_FACE
-        perm = [
-            ((a + p) * n_gy + b + q, a * n_gy + b)
-            for a in range(n_gx) for b in range(n_gy)
-            if 0 <= a + p < n_gx and 0 <= b + q < n_gy
-        ]
-        pieces.append(lax.ppermute(outgoing[:count], ("gx", "gy"), perm))
+    halo = exchange(own, send[0, 0])
     smem = pl.BlockSpec(memory_space=pltpu.SMEM)
     vmem = pl.BlockSpec(memory_space=pltpu.VMEM)
     rates = pl.pallas_call(
         rates_kernel,
         out_shape=jax.ShapeDtypeStruct((TPD, 4, 128), f32),
-        in_specs=[smem] * 3 + [vmem] * 9,
+        in_specs=[smem] * 3 + [vmem] * 2,
         out_specs=vmem,
         scratch_shapes=[
             pltpu.VMEM((7 * 3 * 64, 128), f32),
@@ -228,7 +305,7 @@
             pltpu.SMEM((3,), jnp.int32),
         ],
         compiler_params=pltpu.CompilerParams(vmem_limit_bytes=56 * 2**20),
-    )(heavy_flag[0], order[0, 0], nbr[0, 0].reshape(-1), own, *pieces)
+    )(heavy_flag[0], order[0, 0], nbr[0, 0].reshape(-1), own, halo)
     return rates[None, None]
 
 

time: 203 us -> 183 us (0.901)
  the two profiles are of different devices: /device:TPU:24 before, /device:TPU:32 now
where the time goes in v2:
time: 183 us; the launch traced here: 182 us
  Pallas kernels  176 us (96%)
  local copies, waits for them, and re-layouts  4.46 us (2%)
    pallas_call x1, Pallas kernels, shards(): pl.pallas_call(rates_kernel, out_shape=jax.ShapeDtypeStruct((TPD, 4, 128)...  154 us
    pallas_call x1, Pallas kernels, exchange(): pl.pallas_call(kernel, out_shape=jax.ShapeDtypeStruct((starts()[1], 8, 12...  22.3 us
    unnamed x7, local copies, waits for them, and re-layouts  3.75 us

profile of v2, /device:TPU:32, one launch (start us, length us, event | category | flops | bytes accessed | tf_op | source)
XLA Modules:
  0.0 181.6 jit_solution(12279335075435227878)
XLA Ops:
  0.7 0.8 copy.6
  1.5 0.7 reshape_squeeze.3.nbr
  2.2 0.0 copy-start.1
  2.2 1.2 copy-done.1
  3.4 0.0 copy-start.2
  3.4 0.7 copy-done.2
  4.1 22.3 %shard_map.55.halo = f32[320,8,128]{2,1,0:T(8,128)S(1)} custom-call(s32[64]{0:T(128)S(1)} %bitcast.10, f32[256,8,128]{2,1,0:T(8,128)S(1)} %bitcast.9), custom_call_target="tpu_custom_call" | custom-call | tf_op jit(solution)/shard_map/pallas_call | solution.py:273
  26.4 0.0 copy-start
  26.4 1.1 copy-done
  27.5 154.1 %shard_map.56 = f32[256,4,128]{2,1,0:T(4,128)} custom-call(s32[1]{0:T(128)} %bitcast.7.heavy, s32[256]{0:T(256)} %bitcast.11, s32[2048]{0:T(1024)} %reshape_squeeze.3.nbr, f32[256,8,128]{2,1,0:T(8,128)} %bitcast.8, f32[320,8,128]{2,1,0:T(8,128)} %copy-done), custom_call_target="tpu_custom_call" | custom-call | tf_op jit(solution)/shard_map/pallas_call | solution.py:292
Async XLA Ops:
  2.2 1.2 copy-start.1
  3.4 0.7 copy-start.2
  26.4 1.1 copy-start

commit v3 on v2

--- a/solution.py
+++ b/solution.py
@@ -1,3 +1,4 @@
+import functools
 import math
 
 import jax
@@ -13,6 +14,7 @@
 HS_FACE = 64
 HS_CORNER = 16
 EXT = 576
+HELP = 44
 OFFSETS = ((-1, -1), (-1, 0), (-1, 1), (0, -1), (0, 1), (1, -1), (1, 0), (1, 1))
 
 SLOPE = -5.0 * 21.0 / (16.0 * math.pi)
@@ -133,31 +135,33 @@
     return sums
 
 
-def finish(acc, t, place, out):
+def finish(acc, t, at, place, out):
     totals = [jnp.sum(acc[q].T, 0, keepdims=True) for q in range(5)]
-    out[t, 0:3] = (-2.0 * SLOPE) * (place[t][:3] * totals[3] - jnp.concatenate(totals[:3], 0))
-    out[t, 3:4] = (2.0 * SLOPE) * totals[4]
-
-
-def rates_kernel(heavy, order, nbr, own, halo, out, stage, table, own_stage, own_table, acc, place, lists, counts):
-    stage[...] = jnp.zeros_like(stage)
-    own_stage[...] = jnp.zeros_like(own_stage)
-    live = LIGHT + (TPD - LIGHT) * heavy[0]
-
-    base = 0
-    for src in (own, halo):
-        def build(b, _, src=src, base=base):
-            other_tables(src, b * 8, base + b * 8, stage, table, place)
+    out[at, 0:3] = (-2.0 * SLOPE) * (place[t][:3] * totals[3] - jnp.concatenate(totals[:3], 0))
+    out[at, 3:4] = (2.0 * SLOPE) * totals[4]
+
+
+def rates_kernel(bounds, order, nbr, own, halo, out, stage, table, own_stage, own_table, acc, place, lists, counts, *, by_slot):
+    low, high = bounds[0], bounds[1]
+
+    @pl.when(high > low)
+    def _():
+        stage[...] = jnp.zeros_like(stage)
+        base = 0
+        for src in (own, halo):
+            def build(b, _, src=src, base=base):
+                other_tables(src, b * 8, base + b * 8, stage, table, place)
+                return 0
+
+            lax.fori_loop(0, src.shape[0] // 8, build, 0)
+            base += src.shape[0]
+
+        def build_own(b, _):
+            own_tables(own, b * 8, own_stage, own_table)
             return 0
 
-        lax.fori_loop(0, src.shape[0] // 8, build, 0)
-        base += src.shape[0]
-
-    def build_own(b, _):
-        own_tables(own, b * 8, own_stage, own_table)
-        return 0
-
-    lax.fori_loop(0, TPD // 8, build_own, 0)
+        own_stage[...] = jnp.zeros_like(own_stage)
+        lax.fori_loop(0, TPD // 8, build_own, 0)
 
     for g in range(3):
         counts[g] = 0
@@ -166,25 +170,28 @@
         t = order[s]
         g = jnp.where(nbr[t * NEIGHBOURS + 6] >= 0, 1, 0) + jnp.where(nbr[t * NEIGHBOURS + 7] >= 0, 1, 0)
         n = counts[g]
-        lists[g * TPD + n] = t
+        lists[0, g * TPD + n] = t
+        lists[1, g * TPD + n] = s - low if by_slot else t
         counts[g] = n + 1
         return 0
 
-    lax.fori_loop(0, live, sort, 0)
+    lax.fori_loop(low, high, sort, 0)
 
     def clear(s, _):
         out[order[s]] = jnp.zeros((4, 128), f32)
         return 0
 
-    lax.fori_loop(live, TPD, clear, 0)
+    if not by_slot:
+        lax.fori_loop(high, bounds[2], clear, 0)
 
     for g in range(3):
         n = counts[g]
 
         def tile(s, mine, g=g, n=n):
-            t = lists[g * TPD + s]
-            finish(acc, lists[g * TPD + jnp.maximum(s - 1, 0)], place, out)
-            following = own_side(own_table[lists[g * TPD + jnp.minimum(s + 1, n - 1)]])
+            t = lists[0, g * TPD + s]
+            before = g * TPD + jnp.maximum(s - 1, 0)
+            finish(acc, lists[0, before], lists[1, before], place, out)
+            following = own_side(own_table[lists[0, g * TPD + jnp.minimum(s + 1, n - 1)]])
             entries = [nbr[t * NEIGHBOURS + k] for k in range(6 + g)]
             for q, value in enumerate(tile_sums(mine, entries, table, place)):
                 acc[q] = value
@@ -192,8 +199,53 @@
 
         @pl.when(n > 0)
         def _(tile=tile, g=g, n=n):
-            lax.fori_loop(0, n, tile, own_side(own_table[lists[g * TPD]]))
-            finish(acc, lists[g * TPD + n - 1], place, out)
+            lax.fori_loop(0, n, tile, own_side(own_table[lists[0, g * TPD]]))
+            last = g * TPD + n - 1
+            finish(acc, lists[0, last], lists[1, last], place, out)
+
+
+def rates_of(bounds, order, nbr, own, halo, count, by_slot):
+    smem = pl.BlockSpec(memory_space=pltpu.SMEM)
+    vmem = pl.BlockSpec(memory_space=pltpu.VMEM)
+    return pl.pallas_call(
+        functools.partial(rates_kernel, by_slot=by_slot),
+        out_shape=jax.ShapeDtypeStruct((count, 4, 128), f32),
+        in_specs=[smem] * 3 + [vmem] * 2,
+        out_specs=vmem,
+        scratch_shapes=[
+            pltpu.VMEM((7 * 3 * 64, 128), f32),
+            pltpu.VMEM((EXT, 192, 128), bf16),
+            pltpu.VMEM((2 * 3 * 64, 128), f32),
+            pltpu.VMEM((TPD, 48, 128), f32),
+            pltpu.VMEM((5, 128, 128), f32),
+            pltpu.VMEM((EXT, 8, 128), f32),
+            pltpu.SMEM((2, 3 * TPD), jnp.int32),
+            pltpu.SMEM((3,), jnp.int32),
+        ],
+        compiler_params=pltpu.CompilerParams(vmem_limit_bytes=56 * 2**20),
+        cost_estimate=pl.CostEstimate(flops=count * 8 * 128 * 128 * 1000, bytes_accessed=4 * 2**20, transcendentals=0),
+    )(bounds, order, nbr, own, halo)
+
+
+def merge_kernel(heavy, order, mine, helped, out):
+    out[...] = mine[...]
+
+    def put(s, _):
+        out[order[TPD - HELP + s]] = helped[s]
+        return 0
+
+    lax.fori_loop(0, HELP * heavy[0], put, 0)
+
+
+def merge(heavy, order, mine, helped):
+    smem = pl.BlockSpec(memory_space=pltpu.SMEM)
+    vmem = pl.BlockSpec(memory_space=pltpu.VMEM)
+    return pl.pallas_call(
+        merge_kernel,
+        out_shape=jax.ShapeDtypeStruct((TPD, 4, 128), f32),
+        in_specs=[smem] * 2 + [vmem] * 2,
+        out_specs=vmem,
+    )(heavy, order, mine, helped)
 
 
 def starts():
@@ -285,28 +337,21 @@
 
 
 def shards(state, heavy_flag, order, send, nbr):
-    own = state[0, 0]
+    own, order, nbr = state[0, 0], order[0, 0], nbr[0, 0].reshape(-1)
+    heavy = heavy_flag[0]
+    half = lax.axis_size("gx") // 2
+    partners = [(g, (g + half) % (2 * half)) for g in range(2 * half)]
     halo = exchange(own, send[0, 0])
-    smem = pl.BlockSpec(memory_space=pltpu.SMEM)
-    vmem = pl.BlockSpec(memory_space=pltpu.VMEM)
-    rates = pl.pallas_call(
-        rates_kernel,
-        out_shape=jax.ShapeDtypeStruct((TPD, 4, 128), f32),
-        in_specs=[smem] * 3 + [vmem] * 2,
-        out_specs=vmem,
-        scratch_shapes=[
-            pltpu.VMEM((7 * 3 * 64, 128), f32),
-            pltpu.VMEM((EXT, 192, 128), bf16),
-            pltpu.VMEM((2 * 3 * 64, 128), f32),
-            pltpu.VMEM((TPD, 48, 128), f32),
-            pltpu.VMEM((5, 128, 128), f32),
-            pltpu.VMEM((EXT, 8, 128), f32),
-            pltpu.SMEM((3 * TPD,), jnp.int32),
-            pltpu.SMEM((3,), jnp.int32),
-        ],
-        compiler_params=pltpu.CompilerParams(vmem_limit_bytes=56 * 2**20),
-    )(heavy_flag[0], order[0, 0], nbr[0, 0].reshape(-1), own, halo)
-    return rates[None, None]
+    own_out, halo_out, lists = lax.optimization_barrier((own, halo, jnp.concatenate([order, nbr])))
+    far_own, far_halo, far_lists = (lax.ppermute(v, "gx", partners) for v in (own_out, halo_out, lists))
+    live = LIGHT + (TPD - HELP - LIGHT) * heavy
+    bounds = jnp.concatenate([jnp.zeros_like(live), live, jnp.where(heavy > 0, live, TPD)])
+    mine = rates_of(bounds, order, nbr, own, halo, TPD, False)
+    far_bounds = jnp.concatenate([TPD - HELP * (1 - heavy), jnp.full_like(live, TPD), jnp.full_like(live, TPD)])
+    far_bounds, mine = lax.optimization_barrier((far_bounds, mine))
+    helped = rates_of(far_bounds, far_lists[:TPD], far_lists[TPD:], far_own, far_halo, HELP, True)
+    helped = lax.ppermute(helped, "gx", partners)
+    return merge(heavy, order, mine, helped)[None, None]
 
 
 def solution(mesh):

time: 183 us -> 180 us (0.984); the launches traced: 182 us -> 177 us
  Pallas kernels: 176 us -> 150 us
  starting transfers between devices: 0 us -> 15.2 us
  waiting for transfers between devices: 0 us -> 2.72 us
  local copies, waits for them, and re-layouts: 4.46 us -> 7.16 us
    pallas_call x1 -> x3, Pallas kernels: 154 us -> 128 us  [the longest x2 126 us: rates_of(): pl.pallas_call(functools.partial(rates_kernel, by_slot=by_slot), out_shap...]
    ppermute x0 -> x4, starting transfers between devices: none -> 15.2 us  [the longest x1 11.1 us: shards(): helped = lax.ppermute(helped, 'gx', partners)]
    ppermute x0 -> x4, waiting for transfers between devices: none -> 2.72 us  [the longest x1 2.72 us: shards(): helped = lax.ppermute(helped, 'gx', partners)]
    unnamed x7 -> x19, local copies, waits for them, and re-layouts: 3.75 us -> 5.39 us
  transfers between devices with their start and end apart: 0 -> 4, of which waited for: 0 -> 1; matrix products, arithmetic and copies ran while one was open for 0% -> 1% of each run, Pallas kernels for 0% -> 49%
where the time goes in v3:
time: 180 us; the launch traced here: 177 us
  Pallas kernels  150 us (83%)
  starting transfers between devices  15.2 us (8%)
  local copies, waits for them, and re-layouts  7.16 us (4%)
  waiting for transfers between devices  2.72 us (2%)
    pallas_call x2, Pallas kernels, rates_of(): pl.pallas_call(functools.partial(rates_kernel, by_slot=by_slot), out_shap...  126 us
    pallas_call x1, Pallas kernels, exchange(): pl.pallas_call(kernel, out_shape=jax.ShapeDtypeStruct((starts()[1], 8, 12...  22.3 us
    ppermute x1, starting transfers between devices, shards(): helped = lax.ppermute(helped, 'gx', partners)  11.1 us
    unnamed x19, local copies, waits for them, and re-layouts  5.39 us
    ppermute x3, starting transfers between devices, shards(): lax.ppermute(v, 'gx', partners)  4.11 us
  transfers between devices with their start and end apart: 4, of which 1 were waited for; matrix products, arithmetic and copies ran while one was open for 1% of the time, Pallas kernels for 49%

profile of v3, /device:TPU:32, one launch (start us, length us, event | category | flops | bytes accessed | tf_op | source)
XLA Modules:
  0.0 176.5 jit_solution(205849723739088758)
XLA Ops:
  0.0 0.8 copy.6
  0.8 0.1 reshape_squeeze.3.nbr
  1.0 0.0 copy-start.5
  1.0 0.0 copy-start.1
  1.0 1.2 copy-done.1
  2.2 0.7 copy-done.3
  2.9 22.3 %shard_map.55.halo = f32[320,8,128]{2,1,0:T(8,128)S(1)} custom-call(s32[64]{0:T(128)S(1)} %bitcast.14, f32[256,8,128]{2,1,0:T(8,128)S(1)} %bitcast.12), custom_call_target="tpu_custom_call" | custom-call | tf_op jit(solution)/shard_map/pallas_call | solution.py:325
  25.2 0.6 collective-permute-start
  25.8 3.0 %collective-permute-start.2 = (f32[320,8,128]{2,1,0:T(8,128)S(1)}, f32[320,8,128]{2,1,0:T(8,128)S(1)}, u32[]{:S(2)}, u32[]{:S(2)}) collective-permute-start(f32[320,8,128]{2,1,0:T(8,128)S(1)} %shard_map.55.halo), channel_id=1, source_target_pairs={{0,128},{16,144},{32,160},{48,176},{64,192},{80,208},{96,224},{112... | collective-permute-start | bytes 3932168 | tf_op jit(solution)/shard_map/ppermute | solution.py:346
  28.9 0.5 collective-permute-start.1
  30.0 0.7 pad_add_fusion.1.bounds
  30.7 86.3 %shard_map.56.mine = f32[256,4,128]{2,1,0:T(4,128)} custom-call(s32[3]{0:T(128)} %pad_add_fusion.1.bounds, s32[256]{0:T(256)} %bitcast.15, s32[2048]{0:T(1024)} %copy-done.5, f32[256,8,128]{2,1,0:T(8,128)} %bitcast.11, f32[320,8,128]{2,1,0:T(8,128)} %copy-done), custom_call_target="tpu_custom_call" | custom-call | flops 33554432000 | bytes 4194304 | tf_op jit(solution)/shard_map/pallas_call | solution.py:210
  117.0 0.5 concatenate.9.bounds
  117.5 0.6 slice.9.nbr
  118.1 0.6 slice.8.order
  118.7 0.0 collective-permute-done.1.own
  118.7 0.0 collective-permute-done.2.halo
  118.7 1.0 copy-done.8
  119.7 1.1 copy-done.7
  120.7 39.5 %shard_map.57 = f32[44,4,128]{2,1,0:T(4,128)} custom-call(s32[3]{0:T(128)} %concatenate.9.bounds, s32[256]{0:T(256)} %slice.8.order, s32[2048]{0:T(1024)} %slice.9.nbr, f32[256,8,128]{2,1,0:T(8,128)} %copy-done.8, f32[320,8,128]{2,1,0:T(8,128)} %copy-done.7), custom_call_target="tpu_custom_call" | custom-call | flops 5767168000 | bytes 4194304 | tf_op jit(solution)/shard_map/pallas_call | solution.py:210
  160.2 11.1 %collective-permute-start.3 = (f32[44,4,128]{2,1,0:T(4,128)}, f32[44,4,128]{2,1,0:T(4,128)S(1)}, u32[]{:S(2)}, u32[]{:S(2)}) collective-permute-start(f32[44,4,128]{2,1,0:T(4,128)} %shard_map.57), channel_id=1, source_target_pairs={{0,128},{16,144},{32,160},{48,176},{64,192},{80,208},{96,224},{112... | collective-permute-start | bytes 270344 | tf_op jit(solution)/shard_map/ppermute | solution.py:353
  171.3 2.7 %collective-permute-done.3.helped = f32[44,4,128]{2,1,0:T(4,128)S(1)} collective-permute-done((f32[44,4,128]{2,1,0:T(4,128)}, f32[44,4,128]{2,1,0:T(4,128)S(1)}, u32[]{:S(2)}, u32[]{:S(2)}) %collective-permute-start.3) | collective-permute-done | bytes 90144 | tf_op jit(solution)/shard_map/ppermute | solution.py:353
  174.0 0.6 copy-done.4
  174.7 1.9 %shard_map.58 = f32[256,4,128]{2,1,0:T(4,128)} custom-call(s32[1]{0:T(128)} %bitcast.10.heavy, s32[256]{0:T(256)} %bitcast.16, f32[256,4,128]{2,1,0:T(4,128)} %shard_map.56.mine, f32[44,4,128]{2,1,0:T(4,128)} %copy-done.4), custom_call_target="tpu_custom_call" | custom-call | tf_op jit(solution)/shard_map/pallas_call | solution.py:243
  (13 shorter events, 0.0 us)
Async XLA Ops:
  0.0 25.2 %copy-start.6 = (s32[1,1,256]{2,1,0:T(1,128)S(1)}, s32[1,1,256]{2,1,0:T(1,128)}, u32[]{:S(2)}) copy-start(s32[1,1,256]{2,1,0:T(1,128)} %param.7) | copy-start | bytes 3076
  1.0 29.7 %copy-start.5 = (s32[2048]{0:T(1024)}, s32[2048]{0:T(1024)S(1)}, u32[]{:S(2)}) copy-start(s32[2048]{0:T(1024)S(1)} %reshape_squeeze.3.nbr) | copy-start | bytes 24580
  1.0 1.2 copy-start.1
  2.2 0.7 copy-start.3
  2.9 26.0 %copy-start.2 = (f32[1,1,256,8,128]{4,3,2,1,0:T(8,128)S(1)}, f32[1,1,256,8,128]{4,3,2,1,0:T(8,128)}, u32[]{:S(2)}) copy-start(f32[1,1,256,8,128]{4,3,2,1,0:T(8,128)} %param.5) | copy-start | bytes 3145732
  25.2 5.5 %copy-start = (f32[320,8,128]{2,1,0:T(8,128)}, f32[320,8,128]{2,1,0:T(8,128)S(1)}, u32[]{:S(2)}) copy-start(f32[320,8,128]{2,1,0:T(8,128)S(1)} %shard_map.55.halo) | copy-start | bytes 3932164
  25.2 92.3 %collective-permute-start = (s32[2304]{0:T(1024)S(1)}, s32[2304]{0:T(1024)S(1)}, u32[]{:S(2)}, u32[]{:S(2)}) collective-permute-start(s32[2304]{0:T(1024)S(1)} %pad_add_fusion), channel_id=1, source_target_pairs={{0,128},{16,144},{32,160},{48,176},{64,192},{80,208},{96,224},{112... | collective-permute-start | bytes 27656 | tf_op jit(solution)/shard_map/ppermute | solution.py:346
  25.8 92.9 %collective-permute-start.2 = (f32[320,8,128]{2,1,0:T(8,128)S(1)}, f32[320,8,128]{2,1,0:T(8,128)S(1)}, u32[]{:S(2)}, u32[]{:S(2)}) collective-permute-start(f32[320,8,128]{2,1,0:T(8,128)S(1)} %shard_map.55.halo), channel_id=1, source_target_pairs={{0,128},{16,144},{32,160},{48,176},{64,192},{80,208},{96,224},{112... | collective-permute-start | bytes 3932168 | tf_op jit(solution)/shard_map/ppermute | solution.py:346
  28.9 89.8 %collective-permute-start.1 = (f32[256,8,128]{2,1,0:T(8,128)S(1)}, f32[256,8,128]{2,1,0:T(8,128)S(1)}, u32[]{:S(2)}, u32[]{:S(2)}) collective-permute-start(f32[256,8,128]{2,1,0:T(8,128)S(1)} %bitcast.13), channel_id=1, source_target_pairs={{0,128},{16,144},{32,160},{48,176},{64,192},{80,208},{96,224},{112... | collective-permute-start | bytes 3145736 | tf_op jit(solution)/shard_map/ppermute | solution.py:346
  118.7 1.0 copy-start.8
  119.7 1.1 copy-start.7
  160.2 13.8 %collective-permute-start.3 = (f32[44,4,128]{2,1,0:T(4,128)}, f32[44,4,128]{2,1,0:T(4,128)S(1)}, u32[]{:S(2)}, u32[]{:S(2)}) collective-permute-start(f32[44,4,128]{2,1,0:T(4,128)} %shard_map.57), channel_id=1, source_target_pairs={{0,128},{16,144},{32,160},{48,176},{64,192},{80,208},{96,224},{112... | collective-permute-start | bytes 270344 | tf_op jit(solution)/shard_map/ppermute | solution.py:353
  174.0 0.6 copy-start.4

commit v4 on v3

--- a/solution.py
+++ b/solution.py
@@ -14,7 +14,7 @@
 HS_FACE = 64
 HS_CORNER = 16
 EXT = 576
-HELP = 44
+HELP = 40
 OFFSETS = ((-1, -1), (-1, 0), (-1, 1), (0, -1), (0, 1), (1, -1), (1, 0), (1, 1))
 
 SLOPE = -5.0 * 21.0 / (16.0 * math.pi)
@@ -24,6 +24,8 @@
 OWN_PART = (0, 0, 0, 1, 1, 2)
 OTHER_PART = (0, 1, 2, 0, 1, 0)
 BLOCKS = ((0, 0), (0, 1), (1, 0), (2, 0), (2, 1), (3, 0), (3, 1))
+SIDE = 4
+STAGE = 7 * 3 * 64
 bf16, f32 = jnp.bfloat16, jnp.float32
 
 
@@ -71,22 +73,25 @@
     )
 
 
-def other_tables(src, first, dest, stage, table, place):
+def stage_rows(src, first, stage, at):
     for (q, r), value in other_rows(src, first).items():
         b = BLOCKS.index((q, r // 8))
         for part, v in enumerate(split3(value)):
-            stage[pl.ds(((b * 3 + part) * 8 + r % 8) * 8, 8), :] = v
+            stage[pl.ds(at + ((b * 3 + part) * 8 + r % 8) * 8, 8), :] = v
+
+
+def store_tables(src, first, dest, stage, at, table, place):
     zero = jnp.zeros((8, 128), f32)
     for i in range(8):
         for part in range(3):
             for q in range(4):
                 halves = [
-                    stage[pl.ds((BLOCKS.index((q, h)) * 3 + part) * 64 + i, 8, stride=8), :]
+                    stage[pl.ds(at + (BLOCKS.index((q, h)) * 3 + part) * 64 + i, 8, stride=8), :]
                     if (q, h) in BLOCKS else zero
                     for h in range(2)
                 ]
-                at = part * 64 + q * 16
-                table[dest + i, at:at + 16, :] = jnp.concatenate(halves, 0).astype(bf16)
+                row = part * 64 + q * 16
+                table[dest + i, row:row + 16, :] = jnp.concatenate(halves, 0).astype(bf16)
         place[dest + i] = (src[first + i] - 3.0) * 0.5
 
 
@@ -141,41 +146,61 @@
     out[at, 3:4] = (2.0 * SLOPE) * totals[4]
 
 
-def rates_kernel(bounds, order, nbr, own, halo, out, stage, table, own_stage, own_table, acc, place, lists, counts, *, by_slot):
+def rates_kernel(bounds, order, nbr, ext, out, stage, table, own_stage, own_table, acc, place, lists, blank, sides, *, by_slot):
     low, high = bounds[0], bounds[1]
 
     @pl.when(high > low)
     def _():
         stage[...] = jnp.zeros_like(stage)
-        base = 0
-        for src in (own, halo):
-            def build(b, _, src=src, base=base):
-                other_tables(src, b * 8, base + b * 8, stage, table, place)
-                return 0
-
-            lax.fori_loop(0, src.shape[0] // 8, build, 0)
-            base += src.shape[0]
+        own_stage[...] = jnp.zeros_like(own_stage)
+        blank[...] = jnp.where(lax.broadcasted_iota(jnp.int32, blank.shape, 1) == 6, 1.0, 0.0)
+
+        def build(b, _):
+            for i in range(2):
+                stage_rows(ext, b * 16 + i * 8, stage, i * STAGE)
+            for i in range(2):
+                store_tables(ext, b * 16 + i * 8, b * 16 + i * 8, stage, i * STAGE, table, place)
+            return 0
+
+        lax.fori_loop(0, EXT // 16, build, 0)
+        stage_rows(blank, 0, stage, 0)
+        store_tables(blank, 0, EXT, stage, 0, table, place)
 
         def build_own(b, _):
-            own_tables(own, b * 8, own_stage, own_table)
+            own_tables(ext, b * 8, own_stage, own_table)
             return 0
 
-        own_stage[...] = jnp.zeros_like(own_stage)
         lax.fori_loop(0, TPD // 8, build_own, 0)
 
-    for g in range(3):
-        counts[g] = 0
-
-    def sort(s, _):
-        t = order[s]
-        g = jnp.where(nbr[t * NEIGHBOURS + 6] >= 0, 1, 0) + jnp.where(nbr[t * NEIGHBOURS + 7] >= 0, 1, 0)
-        n = counts[g]
-        lists[0, g * TPD + n] = t
-        lists[1, g * TPD + n] = s - low if by_slot else t
-        counts[g] = n + 1
-        return 0
-
-    lax.fori_loop(low, high, sort, 0)
+    def sort(b, sizes):
+        for i in range(4):
+            s = low + b * 4 + i
+            t = order[s]
+            seven = nbr[t * NEIGHBOURS + 6] >= 0
+            eight = nbr[t * NEIGHBOURS + 7] >= 0
+            n = jnp.where(eight, sizes[2], jnp.where(seven, sizes[1], sizes[0]))
+            at = n + jnp.where(eight, 2 * TPD, jnp.where(seven, TPD, 0))
+            lists[0, at] = t
+            lists[1, at] = s - low if by_slot else t
+            sizes = (
+                jnp.where(seven, sizes[0], sizes[0] + 1),
+                jnp.where(eight, sizes[1], jnp.where(seven, sizes[1] + 1, sizes[1])),
+                jnp.where(eight, sizes[2] + 1, sizes[2]),
+            )
+        return sizes
+
+    none = jnp.int32(0)
+    sizes = list(lax.fori_loop(0, (high - low) // 4, sort, (none, none, none)))
+
+    for g in range(2):
+        odd = lax.rem(sizes[g], SIDE)
+        for i in range(SIDE - 1):
+            @pl.when(i < odd)
+            def _(g=g, i=i):
+                for c in range(2):
+                    lists[c, (g + 1) * TPD + sizes[g + 1] + i] = lists[c, g * TPD + sizes[g] - 1 - i]
+        sizes[g] = sizes[g] - odd
+        sizes[g + 1] = sizes[g + 1] + odd
 
     def clear(s, _):
         out[order[s]] = jnp.zeros((4, 128), f32)
@@ -185,46 +210,64 @@
         lax.fori_loop(high, bounds[2], clear, 0)
 
     for g in range(3):
-        n = counts[g]
-
-        def tile(s, mine, g=g, n=n):
-            t = lists[0, g * TPD + s]
-            before = g * TPD + jnp.maximum(s - 1, 0)
-            finish(acc, lists[0, before], lists[1, before], place, out)
-            following = own_side(own_table[lists[0, g * TPD + jnp.minimum(s + 1, n - 1)]])
-            entries = [nbr[t * NEIGHBOURS + k] for k in range(6 + g)]
-            for q, value in enumerate(tile_sums(mine, entries, table, place)):
-                acc[q] = value
-            return following
+        n = sizes[g]
+        steps = lax.div(n + SIDE - 1, SIDE)
+
+        def look(s, g=g, n=n):
+            found = []
+            for i in range(SIDE):
+                at = g * TPD + jnp.clip(s * SIDE + i, 0, n - 1)
+                t = lists[0, at]
+                entries = [nbr[t * NEIGHBOURS + k] for k in range(6 + g)]
+                entries = [jnp.where(e < 0, EXT, e) for e in entries]
+                found.append((t, lists[1, at], *entries))
+            return tuple(found)
+
+        def step(s, carried, look=look):
+            before, now = carried
+            following = look(s + 1)
+            mine = [sides[i] for i in range(SIDE)]
+            for i in range(SIDE):
+                finish(acc.at[pl.ds(5 * i, 5)], before[i][0], before[i][1], place, out)
+            for i in range(SIDE):
+                for q, value in enumerate(tile_sums(mine[i], now[i][2:], table, place)):
+                    acc[5 * i + q] = value
+            for i in range(SIDE):
+                sides[i] = own_side(own_table[following[i][0]])
+            return tuple(x[:2] for x in now), following
 
         @pl.when(n > 0)
-        def _(tile=tile, g=g, n=n):
-            lax.fori_loop(0, n, tile, own_side(own_table[lists[0, g * TPD]]))
-            last = g * TPD + n - 1
-            finish(acc, lists[0, last], lists[1, last], place, out)
-
-
-def rates_of(bounds, order, nbr, own, halo, count, by_slot):
+        def _(look=look, step=step, steps=steps):
+            first = look(0)
+            for i in range(SIDE):
+                sides[i] = own_side(own_table[first[i][0]])
+            before, _ = lax.fori_loop(0, steps, step, (tuple(x[:2] for x in first), first))
+            for i in range(SIDE):
+                finish(acc.at[pl.ds(5 * i, 5)], before[i][0], before[i][1], place, out)
+
+
+def rates_of(bounds, order, nbr, ext, count, by_slot):
     smem = pl.BlockSpec(memory_space=pltpu.SMEM)
     vmem = pl.BlockSpec(memory_space=pltpu.VMEM)
     return pl.pallas_call(
         functools.partial(rates_kernel, by_slot=by_slot),
         out_shape=jax.ShapeDtypeStruct((count, 4, 128), f32),
-        in_specs=[smem] * 3 + [vmem] * 2,
+        in_specs=[smem] * 3 + [vmem],
         out_specs=vmem,
         scratch_shapes=[
-            pltpu.VMEM((7 * 3 * 64, 128), f32),
-            pltpu.VMEM((EXT, 192, 128), bf16),
+            pltpu.VMEM((2 * STAGE, 128), f32),
+            pltpu.VMEM((EXT + 8, 192, 128), bf16),
             pltpu.VMEM((2 * 3 * 64, 128), f32),
             pltpu.VMEM((TPD, 48, 128), f32),
-            pltpu.VMEM((5, 128, 128), f32),
-            pltpu.VMEM((EXT, 8, 128), f32),
-            pltpu.SMEM((2, 3 * TPD), jnp.int32),
-            pltpu.SMEM((3,), jnp.int32),
+            pltpu.VMEM((5 * SIDE, 128, 128), f32),
+            pltpu.VMEM((EXT + 8, 8, 128), f32),
+            pltpu.SMEM((2, 3 * TPD + SIDE), jnp.int32),
+            pltpu.VMEM((8, 8, 128), f32),
+            pltpu.VMEM((SIDE, 128, 96), bf16),
         ],
         compiler_params=pltpu.CompilerParams(vmem_limit_bytes=56 * 2**20),
         cost_estimate=pl.CostEstimate(flops=count * 8 * 128 * 128 * 1000, bytes_accessed=4 * 2**20, transcendentals=0),
-    )(bounds, order, nbr, own, halo)
+    )(bounds, order, nbr, ext)
 
 
 def merge_kernel(heavy, order, mine, helped, out):
@@ -249,14 +292,14 @@
 
 
 def starts():
-    first, at = [], 0
+    first, at = [], TPD
     for p, q in OFFSETS:
         first.append(at)
         at += HS_CORNER if p and q else HS_FACE
     return first, at
 
 
-def exchange_kernel(n_gx, n_gy, send, own, halo, outgoing, send_sem, recv_sem):
+def exchange_kernel(n_gx, n_gy, send, own, ext, outgoing, send_sem, recv_sem):
     a, b = lax.axis_index("gx"), lax.axis_index("gy")
     first, _ = starts()
 
@@ -289,7 +332,7 @@
         count = HS_CORNER if p and q else HS_FACE
         return pltpu.make_async_remote_copy(
             src_ref=outgoing.at[pl.ds(0, count)],
-            dst_ref=halo.at[pl.ds(first[there], count)],
+            dst_ref=ext.at[pl.ds(first[there], count)],
             send_sem=send_sem.at[i],
             recv_sem=recv_sem.at[there],
             device_id=(a + p, b + q),
@@ -301,12 +344,17 @@
         def _(i=i, p=p, q=q):
             copy(i, OFFSETS.index((-p, -q))).start()
 
+    def keep(b, _):
+        ext[pl.ds(b * 8, 8)] = own[pl.ds(b * 8, 8)]
+        return 0
+
+    lax.fori_loop(0, TPD // 8, keep, 0)
     for i, (p, q) in enumerate(OFFSETS):
         count = HS_CORNER if p and q else HS_FACE
 
         @pl.when(jnp.logical_not(beside(p, q)))
         def _(i=i, count=count):
-            halo[pl.ds(first[i], count)] = jnp.zeros((count, 8, 128), f32)
+            ext[pl.ds(first[i], count)] = jnp.zeros((count, 8, 128), f32)
 
     for i, (p, q) in enumerate(OFFSETS):
         @pl.when(beside(p, q))
@@ -341,15 +389,15 @@
     heavy = heavy_flag[0]
     half = lax.axis_size("gx") // 2
     partners = [(g, (g + half) % (2 * half)) for g in range(2 * half)]
-    halo = exchange(own, send[0, 0])
-    own_out, halo_out, lists = lax.optimization_barrier((own, halo, jnp.concatenate([order, nbr])))
-    far_own, far_halo, far_lists = (lax.ppermute(v, "gx", partners) for v in (own_out, halo_out, lists))
+    ext = exchange(own, send[0, 0])
+    ext_out, lists = lax.optimization_barrier((ext, jnp.concatenate([order, nbr])))
+    far_ext, far_lists = (lax.ppermute(v, "gx", partners) for v in (ext_out, lists))
     live = LIGHT + (TPD - HELP - LIGHT) * heavy
     bounds = jnp.concatenate([jnp.zeros_like(live), live, jnp.where(heavy > 0, live, TPD)])
-    mine = rates_of(bounds, order, nbr, own, halo, TPD, False)
+    mine = rates_of(bounds, order, nbr, ext, TPD, False)
     far_bounds = jnp.concatenate([TPD - HELP * (1 - heavy), jnp.full_like(live, TPD), jnp.full_like(live, TPD)])
     far_bounds, mine = lax.optimization_barrier((far_bounds, mine))
-    helped = rates_of(far_bounds, far_lists[:TPD], far_lists[TPD:], far_own, far_halo, HELP, True)
+    helped = rates_of(far_bounds, far_lists[:TPD], far_lists[TPD:], far_ext, HELP, True)
     helped = lax.ppermute(helped, "gx", partners)
     return merge(heavy, order, mine, helped)[None, None]
 

time: 180 us -> 159 us (0.88); the launches traced: 177 us -> 158 us
  starting transfers between devices: 15.2 us -> 3.62 us
  Pallas kernels: 150 us -> 140 us
  waiting for transfers between devices: 2.72 us -> 6.66 us
    ppermute x1, starting transfers between devices: 11.1 us -> 0.01 us  [shards(): helped = lax.ppermute(helped, 'gx', partners)]
    pallas_call x2, Pallas kernels: 126 us -> 115 us  [rates_of(): pl.pallas_call(functools.partial(rates_kernel, by_slot=by_slot), out_shap...]
    ppermute x1, waiting for transfers between devices: 2.72 us -> 6.65 us  [shards(): helped = lax.ppermute(helped, 'gx', partners)]
    unnamed x19 -> x13, local copies, waits for them, and re-layouts: 5.39 us -> 4.75 us
    ppermute x3 -> x2, starting transfers between devices: 4.11 us -> 3.62 us  [shards(): lax.ppermute(v, 'gx', partners)]
  transfers between devices with their start and end apart: 4 -> 3, of which waited for: 1 -> 1; matrix products, arithmetic and copies ran while one was open for 1% -> 1% of each run, Pallas kernels for 49% -> 71%
where the time goes in v4:
time: 159 us; the launch traced here: 158 us
  Pallas kernels  140 us (88%)
  waiting for transfers between devices  6.66 us (4%)
  local copies, waits for them, and re-layouts  6.56 us (4%)
  starting transfers between devices  3.62 us (2%)
    pallas_call x2, Pallas kernels, rates_of(): pl.pallas_call(functools.partial(rates_kernel, by_slot=by_slot), out_shap...  115 us
    pallas_call x1, Pallas kernels, exchange(): pl.pallas_call(kernel, out_shape=jax.ShapeDtypeStruct((starts()[1], 8, 12...  22.3 us
    ppermute x1, waiting for transfers between devices, shards(): helped = lax.ppermute(helped, 'gx', partners)  6.65 us
    unnamed x13, local copies, waits for them, and re-layouts  4.75 us
    ppermute x2, starting transfers between devices, shards(): lax.ppermute(v, 'gx', partners)  3.62 us
  transfers between devices with their start and end apart: 3, of which 1 were waited for; matrix products, arithmetic and copies ran while one was open for 1% of the time, Pallas kernels for 71%

profile of v4, /device:TPU:32, one launch (start us, length us, event | category | flops | bytes accessed | tf_op | source)
XLA Modules:
  0.0 158.4 jit_solution(10589810855428441231)
XLA Ops:
  0.0 0.8 copy.6
  0.8 0.1 reshape_squeeze.3.nbr
  0.9 0.0 copy-start.4
  0.9 0.7 pad_add_fusion
  1.6 1.2 copy-done.1
  2.9 0.7 copy-done.2
  3.5 22.3 %shard_map.55.ext = f32[576,8,128]{2,1,0:T(8,128)S(1)} custom-call(s32[64]{0:T(128)S(1)} %bitcast.12, f32[256,8,128]{2,1,0:T(8,128)S(1)} %bitcast.11), custom_call_target="tpu_custom_call" | custom-call | tf_op jit(solution)/shard_map/pallas_call | solution.py:373
  25.9 0.0 copy-start
  25.9 0.6 collective-permute-start
  26.5 3.0 %collective-permute-start.1 = (f32[576,8,128]{2,1,0:T(8,128)S(1)}, f32[576,8,128]{2,1,0:T(8,128)S(1)}, u32[]{:S(2)}, u32[]{:S(2)}) collective-permute-start(f32[576,8,128]{2,1,0:T(8,128)S(1)} %shard_map.55.ext), channel_id=1, source_target_pairs={{0,128},{16,144},{32,160},{48,176},{64,192},{80,208},{96,224},{112... | collective-permute-start | bytes 7077896 | tf_op jit(solution)/shard_map/ppermute | solution.py:394
  30.2 0.6 pad_add_fusion.1.bounds
  30.8 0.0 copy-done
  30.8 112.5 %shard_map.56.mine = f32[256,4,128]{2,1,0:T(4,128)} custom-call(s32[3]{0:T(128)} %pad_add_fusion.1.bounds, s32[256]{0:T(256)} %bitcast.14, s32[2048]{0:T(1024)} %copy-done.4, f32[576,8,128]{2,1,0:T(8,128)} %copy-done), custom_call_target="tpu_custom_call" | custom-call | flops 33554432000 | bytes 4194304 | tf_op jit(solution)/shard_map/pallas_call | solution.py:252
  143.2 0.5 concatenate.9.bounds
  143.8 0.0 collective-permute-done
  143.8 0.6 slice.8.order
  144.3 0.6 slice.9.nbr
  144.9 0.0 collective-permute-done.1.ext
  144.9 1.4 copy-done.5
  146.4 2.6 %shard_map.57 = f32[40,4,128]{2,1,0:T(4,128)} custom-call(s32[3]{0:T(128)} %concatenate.9.bounds, s32[256]{0:T(256)} %slice.8.order, s32[2048]{0:T(1024)} %slice.9.nbr, f32[576,8,128]{2,1,0:T(8,128)} %copy-done.5), custom_call_target="tpu_custom_call" | custom-call | flops 5242880000 | bytes 4194304 | tf_op jit(solution)/shard_map/pallas_call | solution.py:252
  148.9 0.0 collective-permute-start.2
  148.9 6.7 %collective-permute-done.2.helped = f32[40,4,128]{2,1,0:T(4,128)S(1)} collective-permute-done((f32[40,4,128]{2,1,0:T(4,128)}, f32[40,4,128]{2,1,0:T(4,128)S(1)}, u32[]{:S(2)}, u32[]{:S(2)}) %collective-permute-start.2) | collective-permute-done | bytes 81952 | tf_op jit(solution)/shard_map/ppermute | solution.py:401
  155.6 0.6 copy-done.3
  156.2 2.1 %shard_map.58 = f32[256,4,128]{2,1,0:T(4,128)} custom-call(s32[1]{0:T(128)} %bitcast.10.heavy, s32[256]{0:T(256)} %bitcast.15, f32[256,4,128]{2,1,0:T(4,128)} %shard_map.56.mine, f32[40,4,128]{2,1,0:T(4,128)} %copy-done.3), custom_call_target="tpu_custom_call" | custom-call | tf_op jit(solution)/shard_map/pallas_call | solution.py:286
  (5 shorter events, 0.0 us)
Async XLA Ops:
  0.9 29.8 %copy-start.4 = (s32[2048]{0:T(1024)}, s32[2048]{0:T(1024)S(1)}, u32[]{:S(2)}) copy-start(s32[2048]{0:T(1024)S(1)} %reshape_squeeze.3.nbr) | copy-start | bytes 24580
  1.6 1.2 copy-start.1
  2.9 0.7 copy-start.2
  25.9 4.9 %copy-start = (f32[576,8,128]{2,1,0:T(8,128)}, f32[576,8,128]{2,1,0:T(8,128)S(1)}, u32[]{:S(2)}) copy-start(f32[576,8,128]{2,1,0:T(8,128)S(1)} %shard_map.55.ext) | copy-start | bytes 7077892
  25.9 117.9 %collective-permute-start = (s32[2304]{0:T(1024)S(1)}, s32[2304]{0:T(1024)S(1)}, u32[]{:S(2)}, u32[]{:S(2)}) collective-permute-start(s32[2304]{0:T(1024)S(1)} %pad_add_fusion), channel_id=1, source_target_pairs={{0,128},{16,144},{32,160},{48,176},{64,192},{80,208},{96,224},{112... | collective-permute-start | bytes 27656 | tf_op jit(solution)/shard_map/ppermute | solution.py:394
  26.5 118.5 %collective-permute-start.1 = (f32[576,8,128]{2,1,0:T(8,128)S(1)}, f32[576,8,128]{2,1,0:T(8,128)S(1)}, u32[]{:S(2)}, u32[]{:S(2)}) collective-permute-start(f32[576,8,128]{2,1,0:T(8,128)S(1)} %shard_map.55.ext), channel_id=1, source_target_pairs={{0,128},{16,144},{32,160},{48,176},{64,192},{80,208},{96,224},{112... | collective-permute-start | bytes 7077896 | tf_op jit(solution)/shard_map/ppermute | solution.py:394
  144.9 1.4 copy-start.5
  148.9 6.7 %collective-permute-start.2 = (f32[40,4,128]{2,1,0:T(4,128)}, f32[40,4,128]{2,1,0:T(4,128)S(1)}, u32[]{:S(2)}, u32[]{:S(2)}) collective-permute-start(f32[40,4,128]{2,1,0:T(4,128)} %shard_map.57), channel_id=1, source_target_pairs={{0,128},{16,144},{32,160},{48,176},{64,192},{80,208},{96,224},{112... | collective-permute-start | bytes 245768 | tf_op jit(solution)/shard_map/ppermute | solution.py:401
  155.6 0.6 copy-start.3

commit v5 on v4

--- a/solution.py
+++ b/solution.py
@@ -14,7 +14,7 @@
 HS_FACE = 64
 HS_CORNER = 16
 EXT = 576
-HELP = 40
+HELP = 48
 OFFSETS = ((-1, -1), (-1, 0), (-1, 1), (0, -1), (0, 1), (1, -1), (1, 0), (1, 1))
 
 SLOPE = -5.0 * 21.0 / (16.0 * math.pi)
@@ -23,9 +23,9 @@
 SOFT = 0.01 / 4.0
 OWN_PART = (0, 0, 0, 1, 1, 2)
 OTHER_PART = (0, 1, 2, 0, 1, 0)
-BLOCKS = ((0, 0), (0, 1), (1, 0), (2, 0), (2, 1), (3, 0), (3, 1))
+BLOCKS = ((0, 0), (1, 0), (2, 0), (2, 1))
 SIDE = 4
-STAGE = 7 * 3 * 64
+STAGE = 5 * 64
 bf16, f32 = jnp.bfloat16, jnp.float32
 
 
@@ -56,12 +56,12 @@
     gr = GAMMA * rho
     g2 = 2.0 * GAMMA
     return {
-        (0, 3): 2.0 * x, (0, 4): 2.0 * y, (0, 5): 2.0 * z, (0, 7): xx, (0, 8): one,
+        (0, 3): 2.0 * x, (0, 4): 2.0 * y, (0, 5): 2.0 * z, (0, 7): xx,
         (1, 0): m * x, (1, 1): m * y, (1, 2): m * z, (1, 3): m * u, (1, 4): m * v, (1, 5): m * w,
         (1, 6): m, (1, 7): m * vx,
         (2, 3): 2.0 * gr * x, (2, 4): 2.0 * gr * y, (2, 5): 2.0 * gr * z, (2, 7): gr * (xx + SOFT), (2, 8): gr,
         (2, 9): g2 * x, (2, 10): g2 * y, (2, 11): g2 * z, (2, 12): GAMMA * one, (2, 13): GAMMA * xx,
-        (3, 7): m * p, (3, 14): m,
+        (3, 7): m * p, (3, 6): m,
     }
 
 
@@ -75,35 +75,38 @@
 
 def stage_rows(src, first, stage, at):
     for (q, r), value in other_rows(src, first).items():
-        b = BLOCKS.index((q, r // 8))
-        for part, v in enumerate(split3(value)):
-            stage[pl.ds(at + ((b * 3 + part) * 8 + r % 8) * 8, 8), :] = v
+        b, i = (len(BLOCKS), r) if q == 3 else (BLOCKS.index((q, r // 8)), r % 8)
+        stage[pl.ds(at + (b * 8 + i) * 8, 8), :] = value
 
 
 def store_tables(src, first, dest, stage, at, table, place):
     zero = jnp.zeros((8, 128), f32)
+    row = lax.broadcasted_iota(jnp.int32, (8, 128), 0)
+    one = jnp.where(row == 0, 1.0, 0.0)
     for i in range(8):
+        blocks = [split3(stage[pl.ds(at + b * 64 + i, 8, stride=8), :]) for b in range(len(BLOCKS) + 1)]
         for part in range(3):
+            h, c, d, d_end, a = (block[part] for block in blocks)
+            halves = (
+                (h, zero if part else one),
+                (c, zero),
+                (d, d_end),
+                (jnp.where(row == 7, a, 0.0), jnp.where(row == 6, a, 0.0)),
+            )
             for q in range(4):
-                halves = [
-                    stage[pl.ds(at + (BLOCKS.index((q, h)) * 3 + part) * 64 + i, 8, stride=8), :]
-                    if (q, h) in BLOCKS else zero
-                    for h in range(2)
-                ]
-                row = part * 64 + q * 16
-                table[dest + i, row:row + 16, :] = jnp.concatenate(halves, 0).astype(bf16)
+                to = part * 64 + q * 16
+                table[dest + i, to:to + 16, :] = jnp.concatenate(halves[q], 0).astype(bf16)
         place[dest + i] = (src[first + i] - 3.0) * 0.5
 
 
 def own_tables(src, first, stage, table):
     for r, value in enumerate(own_rows(src, first)):
-        for part, v in enumerate(split3(value)):
-            stage[pl.ds((((r // 8) * 3 + part) * 8 + r % 8) * 8, 8), :] = v
+        stage[pl.ds(r * 8, 8), :] = value
     for i in range(8):
-        for part in range(3):
-            for h in range(2):
+        for h in range(2):
+            for part, v in enumerate(split3(stage[pl.ds(h * 64 + i, 8, stride=8), :])):
                 at = part * 16 + h * 8
-                table[first + i, at:at + 8, :] = stage[pl.ds((h * 3 + part) * 64 + i, 8, stride=8), :]
+                table[first + i, at:at + 8, :] = v
 
 
 def own_side(rows):
@@ -146,22 +149,27 @@
     out[at, 3:4] = (2.0 * SLOPE) * totals[4]
 
 
-def rates_kernel(bounds, order, nbr, ext, out, stage, table, own_stage, own_table, acc, place, lists, blank, sides, *, by_slot):
+def rates_kernel(bounds, order, nbr, source, out, ext, stage, table, own_stage, own_table, acc, place, lists, blank, sides, sem, *, by_slot):
     low, high = bounds[0], bounds[1]
 
     @pl.when(high > low)
     def _():
+        fetch = pltpu.make_async_copy(source, ext, sem)
+        fetch.start()
         stage[...] = jnp.zeros_like(stage)
         own_stage[...] = jnp.zeros_like(own_stage)
         blank[...] = jnp.where(lax.broadcasted_iota(jnp.int32, blank.shape, 1) == 6, 1.0, 0.0)
 
+        fetch.wait()
+
         def build(b, _):
-            for i in range(2):
-                stage_rows(ext, b * 16 + i * 8, stage, i * STAGE)
-            for i in range(2):
-                store_tables(ext, b * 16 + i * 8, b * 16 + i * 8, stage, i * STAGE, table, place)
+            stage_rows(ext, b * 16 + 8, stage, STAGE)
+            store_tables(ext, b * 16, b * 16, stage, 0, table, place)
+            stage_rows(ext, jnp.minimum(b * 16 + 16, EXT - 8), stage, 0)
+            store_tables(ext, b * 16 + 8, b * 16 + 8, stage, STAGE, table, place)
             return 0
 
+        stage_rows(ext, 0, stage, 0)
         lax.fori_loop(0, EXT // 16, build, 0)
         stage_rows(blank, 0, stage, 0)
         store_tables(blank, 0, EXT, stage, 0, table, place)
@@ -252,18 +260,20 @@
     return pl.pallas_call(
         functools.partial(rates_kernel, by_slot=by_slot),
         out_shape=jax.ShapeDtypeStruct((count, 4, 128), f32),
-        in_specs=[smem] * 3 + [vmem],
+        in_specs=[smem] * 3 + [pl.BlockSpec(memory_space=pl.ANY)],
         out_specs=vmem,
         scratch_shapes=[
+            pltpu.VMEM((EXT, 8, 128), f32),
             pltpu.VMEM((2 * STAGE, 128), f32),
             pltpu.VMEM((EXT + 8, 192, 128), bf16),
-            pltpu.VMEM((2 * 3 * 64, 128), f32),
+            pltpu.VMEM((2 * 64, 128), f32),
             pltpu.VMEM((TPD, 48, 128), f32),
             pltpu.VMEM((5 * SIDE, 128, 128), f32),
             pltpu.VMEM((EXT + 8, 8, 128), f32),
             pltpu.SMEM((2, 3 * TPD + SIDE), jnp.int32),
             pltpu.VMEM((8, 8, 128), f32),
             pltpu.VMEM((SIDE, 128, 96), bf16),
+            pltpu.SemaphoreType.DMA,
         ],
         compiler_params=pltpu.CompilerParams(vmem_limit_bytes=56 * 2**20),
         cost_estimate=pl.CostEstimate(flops=count * 8 * 128 * 128 * 1000, bytes_accessed=4 * 2**20, transcendentals=0),

time: 159 us -> 150 us (0.943)
  Pallas kernels: 140 us -> 131 us
    pallas_call x2, Pallas kernels: 115 us -> 106 us  [rates_of(): pl.pallas_call(functools.partial(rates_kernel, by_slot=by_slot), out_shap...]
  transfers between devices with their start and end apart: 3 -> 3, of which waited for: 1 -> 1; matrix products, arithmetic and copies ran while one was open for 1% -> 2% of each run, Pallas kernels for 71% -> 70%
where the time goes in v5:
time: 150 us
  Pallas kernels  131 us (87%)
  waiting for transfers between devices  7.03 us (5%)
  local copies, waits for them, and re-layouts  6.56 us (4%)
  starting transfers between devices  3.71 us (2%)
    pallas_call x2, Pallas kernels, rates_of(): pl.pallas_call(functools.partial(rates_kernel, by_slot=by_slot), out_shap...  106 us
    pallas_call x1, Pallas kernels, exchange(): pl.pallas_call(kernel, out_shape=jax.ShapeDtypeStruct((starts()[1], 8, 12...  22.3 us
    ppermute x1, waiting for transfers between devices, shards(): helped = lax.ppermute(helped, 'gx', partners)  7.02 us
    unnamed x13, local copies, waits for them, and re-layouts  4.75 us
    ppermute x2, starting transfers between devices, shards(): lax.ppermute(v, 'gx', partners)  3.62 us
  transfers between devices with their start and end apart: 3, of which 1 were waited for; matrix products, arithmetic and copies ran while one was open for 2% of the time, Pallas kernels for 70%

profile of v5, /device:TPU:32, one launch (start us, length us, event | category | flops | bytes accessed | tf_op | source)
XLA Modules:
  0.0 150.0 jit_solution(7872717939489406695)
XLA Ops:
  0.0 0.8 copy.6
  0.8 0.1 reshape_squeeze.3.nbr
  0.9 0.0 copy-start.4
  0.9 0.7 pad_add_fusion
  1.6 1.2 copy-done.1
  2.9 0.7 copy-done.2
  3.5 22.3 %shard_map.55.source = f32[576,8,128]{2,1,0:T(8,128)S(1)} custom-call(s32[64]{0:T(128)S(1)} %bitcast.12, f32[256,8,128]{2,1,0:T(8,128)S(1)} %bitcast.11), custom_call_target="tpu_custom_call" | custom-call | tf_op jit(solution)/shard_map/pallas_call | solution.py:383
  25.9 0.0 copy-start
  25.9 0.6 collective-permute-start
  26.5 3.0 %collective-permute-start.1 = (f32[576,8,128]{2,1,0:T(8,128)S(1)}, f32[576,8,128]{2,1,0:T(8,128)S(1)}, u32[]{:S(2)}, u32[]{:S(2)}) collective-permute-start(f32[576,8,128]{2,1,0:T(8,128)S(1)} %shard_map.55.source), channel_id=1, source_target_pairs={{0,128},{16,144},{32,160},{48,176},{64,192},{80,208},{96,224},{112... | collective-permute-start | bytes 7077896 | tf_op jit(solution)/shard_map/ppermute | solution.py:404
  30.2 0.6 pad_add_fusion.1.bounds
  30.8 0.0 copy-done
  30.8 104.4 %shard_map.56.mine = f32[256,4,128]{2,1,0:T(4,128)} custom-call(s32[3]{0:T(128)} %pad_add_fusion.1.bounds, s32[256]{0:T(256)} %bitcast.14, s32[2048]{0:T(1024)} %copy-done.4, f32[576,8,128]{2,1,0:T(8,128)} %copy-done), custom_call_target="tpu_custom_call" | custom-call | flops 33554432000 | bytes 4194304 | tf_op jit(solution)/shard_map/pallas_call | solution.py:260
  135.2 0.5 concatenate.9.bounds
  135.7 0.0 collective-permute-done
  135.7 0.6 slice.8.order
  136.3 0.6 slice.9.nbr
  136.9 0.0 collective-permute-done.1.source
  136.9 1.4 copy-done.5
  138.3 1.7 %shard_map.57 = f32[48,4,128]{2,1,0:T(4,128)} custom-call(s32[3]{0:T(128)} %concatenate.9.bounds, s32[256]{0:T(256)} %slice.8.order, s32[2048]{0:T(1024)} %slice.9.nbr, f32[576,8,128]{2,1,0:T(8,128)} %copy-done.5), custom_call_target="tpu_custom_call" | custom-call | flops 6291456000 | bytes 4194304 | tf_op jit(solution)/shard_map/pallas_call | solution.py:260
  140.0 0.1 collective-permute-start.2
  140.1 7.0 %collective-permute-done.2.helped = f32[48,4,128]{2,1,0:T(4,128)S(1)} collective-permute-done((f32[48,4,128]{2,1,0:T(4,128)}, f32[48,4,128]{2,1,0:T(4,128)S(1)}, u32[]{:S(2)}, u32[]{:S(2)}) %collective-permute-start.2) | collective-permute-done | bytes 98336 | tf_op jit(solution)/shard_map/ppermute | solution.py:411
  147.2 0.6 copy-done.3
  147.8 2.2 %shard_map.58 = f32[256,4,128]{2,1,0:T(4,128)} custom-call(s32[1]{0:T(128)} %bitcast.10.heavy, s32[256]{0:T(256)} %bitcast.15, f32[256,4,128]{2,1,0:T(4,128)} %shard_map.56.mine, f32[48,4,128]{2,1,0:T(4,128)} %copy-done.3), custom_call_target="tpu_custom_call" | custom-call | tf_op jit(solution)/shard_map/pallas_call | solution.py:296
  (5 shorter events, 0.0 us)
Async XLA Ops:
  0.9 29.8 %copy-start.4 = (s32[2048]{0:T(1024)}, s32[2048]{0:T(1024)S(1)}, u32[]{:S(2)}) copy-start(s32[2048]{0:T(1024)S(1)} %reshape_squeeze.3.nbr) | copy-start | bytes 24580
  1.6 1.2 copy-start.1
  2.9 0.7 copy-start.2
  25.9 4.9 %copy-start = (f32[576,8,128]{2,1,0:T(8,128)}, f32[576,8,128]{2,1,0:T(8,128)S(1)}, u32[]{:S(2)}) copy-start(f32[576,8,128]{2,1,0:T(8,128)S(1)} %shard_map.55.source) | copy-start | bytes 7077892
  25.9 109.8 %collective-permute-start = (s32[2304]{0:T(1024)S(1)}, s32[2304]{0:T(1024)S(1)}, u32[]{:S(2)}, u32[]{:S(2)}) collective-permute-start(s32[2304]{0:T(1024)S(1)} %pad_add_fusion), channel_id=1, source_target_pairs={{0,128},{16,144},{32,160},{48,176},{64,192},{80,208},{96,224},{112... | collective-permute-start | bytes 27656 | tf_op jit(solution)/shard_map/ppermute | solution.py:404
  26.5 110.4 %collective-permute-start.1 = (f32[576,8,128]{2,1,0:T(8,128)S(1)}, f32[576,8,128]{2,1,0:T(8,128)S(1)}, u32[]{:S(2)}, u32[]{:S(2)}) collective-permute-start(f32[576,8,128]{2,1,0:T(8,128)S(1)} %shard_map.55.source), channel_id=1, source_target_pairs={{0,128},{16,144},{32,160},{48,176},{64,192},{80,208},{96,224},{112... | collective-permute-start | bytes 7077896 | tf_op jit(solution)/shard_map/ppermute | solution.py:404
  136.9 1.4 copy-start.5
  140.0 7.1 %collective-permute-start.2 = (f32[48,4,128]{2,1,0:T(4,128)}, f32[48,4,128]{2,1,0:T(4,128)S(1)}, u32[]{:S(2)}, u32[]{:S(2)}) collective-permute-start(f32[48,4,128]{2,1,0:T(4,128)} %shard_map.57), channel_id=1, source_target_pairs={{0,128},{16,144},{32,160},{48,176},{64,192},{80,208},{96,224},{112... | collective-permute-start | bytes 294920 | tf_op jit(solution)/shard_map/ppermute | solution.py:411
  147.2 0.6 copy-start.3

commit v6 on v5

--- a/solution.py
+++ b/solution.py
@@ -24,7 +24,7 @@
 OWN_PART = (0, 0, 0, 1, 1, 2)
 OTHER_PART = (0, 1, 2, 0, 1, 0)
 BLOCKS = ((0, 0), (1, 0), (2, 0), (2, 1))
-SIDE = 4
+SIDE = 6
 STAGE = 5 * 64
 bf16, f32 = jnp.bfloat16, jnp.float32
 
@@ -275,7 +275,7 @@
             pltpu.VMEM((SIDE, 128, 96), bf16),
             pltpu.SemaphoreType.DMA,
         ],
-        compiler_params=pltpu.CompilerParams(vmem_limit_bytes=56 * 2**20),
+        compiler_params=pltpu.CompilerParams(vmem_limit_bytes=62 * 2**20),
         cost_estimate=pl.CostEstimate(flops=count * 8 * 128 * 128 * 1000, bytes_accessed=4 * 2**20, transcendentals=0),
     )(bounds, order, nbr, ext)
 
@@ -392,6 +392,36 @@
         ],
         compiler_params=pltpu.CompilerParams(collective_id=0, has_side_effects=True, vmem_limit_bytes=8 * 2**20),
     )(send, own)
+
+
+def swap_kernel(half, mine, theirs, send_sem, recv_sem):
+    a, b = lax.axis_index("gx"), lax.axis_index("gy")
+    partner = (lax.rem(a + half, 2 * half), b)
+    barrier = pltpu.get_barrier_semaphore()
+    pl.semaphore_signal(barrier, inc=1, device_id=partner, device_id_type=pl.DeviceIdType.MESH)
+    pl.semaphore_wait(barrier, 1)
+    copy = pltpu.make_async_remote_copy(
+        src_ref=mine,
+        dst_ref=theirs,
+        send_sem=send_sem,
+        recv_sem=recv_sem,
+        device_id=partner,
+        device_id_type=pl.DeviceIdType.MESH,
+    )
+    copy.start()
+    copy.wait()
+
+
+def swap(mine, half):
+    vmem = pl.BlockSpec(memory_space=pltpu.VMEM)
+    return pl.pallas_call(
+        functools.partial(swap_kernel, half),
+        out_shape=jax.ShapeDtypeStruct(mine.shape, mine.dtype),
+        in_specs=[vmem],
+        out_specs=vmem,
+        scratch_shapes=[pltpu.SemaphoreType.DMA, pltpu.SemaphoreType.DMA],
+        compiler_params=pltpu.CompilerParams(collective_id=1, has_side_effects=True),
+    )(mine)
 
 
 def shards(state, heavy_flag, order, send, nbr):
@@ -408,7 +438,7 @@
     far_bounds = jnp.concatenate([TPD - HELP * (1 - heavy), jnp.full_like(live, TPD), jnp.full_like(live, TPD)])
     far_bounds, mine = lax.optimization_barrier((far_bounds, mine))
     helped = rates_of(far_bounds, far_lists[:TPD], far_lists[TPD:], far_ext, HELP, True)
-    helped = lax.ppermute(helped, "gx", partners)
+    helped = swap(helped, half)
     return merge(heavy, order, mine, helped)[None, None]
 
 

time: 150 us -> 152 us (1.013); the launches traced: 150 us -> 150 us
  Pallas kernels: 131 us -> 140 us
  waiting for transfers between devices: 7.03 us -> 0.01 us
  local copies, waits for them, and re-layouts: 6.56 us -> 4.52 us
    pallas_call x0 -> x1, Pallas kernels: none -> 7.95 us  [swap(): pl.pallas_call(functools.partial(swap_kernel, half), out_shape=jax.ShapeD...]
    ppermute x1 -> x0, waiting for transfers between devices: 7.02 us -> none  [shards(): helped = lax.ppermute(helped, 'gx', partners)]
    unnamed x13 -> x7, local copies, waits for them, and re-layouts: 4.75 us -> 2.7 us
  transfers between devices with their start and end apart: 3 -> 2, of which waited for: 1 -> 0; matrix products, arithmetic and copies ran while one was open for 2% -> 2% of each run, Pallas kernels for 70% -> 69%
where the time goes in v6:
time: 152 us; the launch traced here: 150 us
  Pallas kernels  140 us (92%)
  local copies, waits for them, and re-layouts  4.52 us (3%)
  starting transfers between devices  3.62 us (2%)
    pallas_call x2, Pallas kernels, rates_of(): pl.pallas_call(functools.partial(rates_kernel, by_slot=by_slot), out_shap...  106 us
    pallas_call x1, Pallas kernels, exchange(): pl.pallas_call(kernel, out_shape=jax.ShapeDtypeStruct((starts()[1], 8, 12...  23.8 us
    pallas_call x1, Pallas kernels, swap(): pl.pallas_call(functools.partial(swap_kernel, half), out_shape=jax.ShapeD...  7.95 us
    ppermute x2, starting transfers between devices, shards(): lax.ppermute(v, 'gx', partners)  3.62 us
  transfers between devices with their start and end apart: 2, of which 0 were waited for; matrix products, arithmetic and copies ran while one was open for 2% of the time, Pallas kernels for 69%

profile of v6, /device:TPU:32, one launch (start us, length us, event | category | flops | bytes accessed | tf_op | source)
XLA Modules:
  0.0 150.1 jit_solution(10692227165405359278)
XLA Ops:
  0.0 0.8 copy.6
  0.8 0.1 reshape_squeeze.3.nbr
  0.9 0.0 copy-start.2
  0.9 0.7 pad_add_fusion
  1.6 0.0 copy-start
  1.6 1.2 copy-done
  2.9 0.0 copy-start.1
  2.9 0.7 copy-done.1
  3.5 23.8 %shard_map.55.source = f32[576,8,128]{2,1,0:T(8,128)} custom-call(s32[64]{0:T(128)S(1)} %bitcast.12, f32[256,8,128]{2,1,0:T(8,128)S(1)} %bitcast.11), custom_call_target="tpu_custom_call" | custom-call | tf_op jit(solution)/shard_map/pallas_call | solution.py:383
  27.3 0.6 collective-permute-start
  27.9 3.0 %collective-permute-start.1 = (f32[576,8,128]{2,1,0:T(8,128)}, f32[576,8,128]{2,1,0:T(8,128)}, u32[]{:S(2)}, u32[]{:S(2)}) collective-permute-start(f32[576,8,128]{2,1,0:T(8,128)} %shard_map.55.source), channel_id=1, source_target_pairs={{0,128},{16,144},{32,160},{48,176},{64,192},{80,208},{96,224},{112... | collective-permute-start | bytes 7077896 | tf_op jit(solution)/shard_map/ppermute | solution.py:434
  31.6 0.6 pad_add_fusion.1.bounds
  32.2 0.0 copy-done.2
  32.2 104.3 %shard_map.56.mine = f32[256,4,128]{2,1,0:T(4,128)} custom-call(s32[3]{0:T(128)} %pad_add_fusion.1.bounds, s32[256]{0:T(256)} %bitcast.14, s32[2048]{0:T(1024)} %copy-done.2, f32[576,8,128]{2,1,0:T(8,128)} %shard_map.55.source), custom_call_target="tpu_custom_call" | custom-call | flops 33554432000 | bytes 4194304 | tf_op jit(solution)/shard_map/pallas_call | solution.py:260
  136.5 0.5 concatenate.9.bounds
  137.0 0.0 collective-permute-done
  137.0 0.6 slice.8.order
  137.6 0.6 slice.9.nbr
  138.2 0.0 collective-permute-done.1.source
  138.2 1.8 %shard_map.57.mine = f32[48,4,128]{2,1,0:T(4,128)} custom-call(s32[3]{0:T(128)} %concatenate.9.bounds, s32[256]{0:T(256)} %slice.8.order, s32[2048]{0:T(1024)} %slice.9.nbr, f32[576,8,128]{2,1,0:T(8,128)} %collective-permute-done.1.source), custom_call_target="tpu_custom_call" | custom-call | flops 6291456000 | bytes 4194304 | tf_op jit(solution)/shard_map/pallas_call | solution.py:260
  140.0 7.9 %shard_map.58.helped = f32[48,4,128]{2,1,0:T(4,128)} custom-call(f32[48,4,128]{2,1,0:T(4,128)} %shard_map.57.mine), custom_call_target="tpu_custom_call" | custom-call | tf_op jit(solution)/shard_map/pallas_call | solution.py:417
  147.9 2.2 %shard_map.59 = f32[256,4,128]{2,1,0:T(4,128)} custom-call(s32[1]{0:T(128)} %bitcast.10.heavy, s32[256]{0:T(256)} %bitcast.15, f32[256,4,128]{2,1,0:T(4,128)} %shard_map.56.mine, f32[48,4,128]{2,1,0:T(4,128)} %shard_map.58.helped), custom_call_target="tpu_custom_call" | custom-call | tf_op jit(solution)/shard_map/pallas_call | solution.py:296
Async XLA Ops:
  0.9 31.2 %copy-start.2 = (s32[2048]{0:T(1024)}, s32[2048]{0:T(1024)S(1)}, u32[]{:S(2)}) copy-start(s32[2048]{0:T(1024)S(1)} %reshape_squeeze.3.nbr) | copy-start | bytes 24580
  1.6 1.2 copy-start
  2.9 0.7 copy-start.1
  27.3 109.7 %collective-permute-start = (s32[2304]{0:T(1024)S(1)}, s32[2304]{0:T(1024)S(1)}, u32[]{:S(2)}, u32[]{:S(2)}) collective-permute-start(s32[2304]{0:T(1024)S(1)} %pad_add_fusion), channel_id=1, source_target_pairs={{0,128},{16,144},{32,160},{48,176},{64,192},{80,208},{96,224},{112... | collective-permute-start | bytes 27656 | tf_op jit(solution)/shard_map/ppermute | solution.py:434
  27.9 110.3 %collective-permute-start.1 = (f32[576,8,128]{2,1,0:T(8,128)}, f32[576,8,128]{2,1,0:T(8,128)}, u32[]{:S(2)}, u32[]{:S(2)}) collective-permute-start(f32[576,8,128]{2,1,0:T(8,128)} %shard_map.55.source), channel_id=1, source_target_pairs={{0,128},{16,144},{32,160},{48,176},{64,192},{80,208},{96,224},{112... | collective-permute-start | bytes 7077896 | tf_op jit(solution)/shard_map/ppermute | solution.py:434

commit v7 on v6

--- a/solution.py
+++ b/solution.py
@@ -24,7 +24,7 @@
 OWN_PART = (0, 0, 0, 1, 1, 2)
 OTHER_PART = (0, 1, 2, 0, 1, 0)
 BLOCKS = ((0, 0), (1, 0), (2, 0), (2, 1))
-SIDE = 6
+SIDE = 4
 STAGE = 5 * 64
 bf16, f32 = jnp.bfloat16, jnp.float32
 
@@ -309,7 +309,7 @@
     return first, at
 
 
-def exchange_kernel(n_gx, n_gy, send, own, ext, outgoing, send_sem, recv_sem):
+def exchange_kernel(n_gx, n_gy, send, source, ext, own, outgoing, fetch_sem, send_sem, recv_sem):
     a, b = lax.axis_index("gx"), lax.axis_index("gy")
     first, _ = starts()
 
@@ -322,6 +322,8 @@
                 inside = inside & (at < count - 1)
         return inside
 
+    fetch = pltpu.make_async_copy(source, own, fetch_sem)
+    fetch.start()
     barrier = pltpu.get_barrier_semaphore()
     for p, q in OFFSETS:
         @pl.when(beside(p, q))
@@ -332,6 +334,7 @@
         outgoing[s] = own[send[s]]
         return 0
 
+    fetch.wait()
     lax.fori_loop(0, HS_FACE, pick, 0)
     rows = 1 + jnp.where(a > 0, 1, 0) + jnp.where(a < n_gx - 1, 1, 0)
     cols = 1 + jnp.where(b > 0, 1, 0) + jnp.where(b < n_gy - 1, 1, 0)
@@ -383,14 +386,16 @@
     return pl.pallas_call(
         kernel,
         out_shape=jax.ShapeDtypeStruct((starts()[1], 8, 128), f32),
-        in_specs=[pl.BlockSpec(memory_space=pltpu.SMEM), vmem],
+        in_specs=[pl.BlockSpec(memory_space=pltpu.SMEM), pl.BlockSpec(memory_space=pl.ANY)],
         out_specs=vmem,
         scratch_shapes=[
+            pltpu.VMEM((TPD, 8, 128), f32),
             pltpu.VMEM((HS_FACE, 8, 128), f32),
+            pltpu.SemaphoreType.DMA,
             pltpu.SemaphoreType.DMA((8,)),
             pltpu.SemaphoreType.DMA((8,)),
         ],
-        compiler_params=pltpu.CompilerParams(collective_id=0, has_side_effects=True, vmem_limit_bytes=8 * 2**20),
+        compiler_params=pltpu.CompilerParams(collective_id=0, has_side_effects=True, vmem_limit_bytes=62 * 2**20),
     )(send, own)
 
 

time: 152 us -> 150 us (0.987)
  local copies, waits for them, and re-layouts: 4.52 us -> 2.59 us
    unnamed x7 -> x3, local copies, waits for them, and re-layouts: 2.7 us -> 0.82 us
  transfers between devices with their start and end apart: 2 -> 2, of which waited for: 0 -> 0; matrix products, arithmetic and copies ran while one was open for 2% -> 1% of each run, Pallas kernels for 69% -> 71%
where the time goes in v7:
time: 150 us; the launch traced here: 149 us
  Pallas kernels  141 us (94%)
  starting transfers between devices  3.62 us (2%)
  local copies, waits for them, and re-layouts  2.59 us (2%)
    pallas_call x2, Pallas kernels, rates_of(): pl.pallas_call(functools.partial(rates_kernel, by_slot=by_slot), out_shap...  107 us
    pallas_call x1, Pallas kernels, exchange(): pl.pallas_call(kernel, out_shape=jax.ShapeDtypeStruct((starts()[1], 8, 12...  23.9 us
    pallas_call x1, Pallas kernels, swap(): pl.pallas_call(functools.partial(swap_kernel, half), out_shape=jax.ShapeD...  7.79 us
    ppermute x2, starting transfers between devices, shards(): lax.ppermute(v, 'gx', partners)  3.62 us
  transfers between devices with their start and end apart: 2, of which 0 were waited for; matrix products, arithmetic and copies ran while one was open for 1% of the time, Pallas kernels for 71%

profile of v7, /device:TPU:32, one launch (start us, length us, event | category | flops | bytes accessed | tf_op | source)
XLA Modules:
  0.0 149.4 jit_solution(11146804545865824690)
XLA Ops:
  0.0 0.8 copy.6
  0.8 0.1 reshape_squeeze.3.nbr
  0.9 0.0 copy-start
  0.9 0.7 pad_add_fusion
  1.6 23.9 %shard_map.55.source = f32[576,8,128]{2,1,0:T(8,128)} custom-call(s32[64]{0:T(128)} %bitcast.15, f32[256,8,128]{2,1,0:T(8,128)} %bitcast.11), custom_call_target="tpu_custom_call" | custom-call | tf_op jit(solution)/shard_map/pallas_call | solution.py:386
  25.5 0.6 collective-permute-start
  26.1 3.0 %collective-permute-start.1 = (f32[576,8,128]{2,1,0:T(8,128)}, f32[576,8,128]{2,1,0:T(8,128)}, u32[]{:S(2)}, u32[]{:S(2)}) collective-permute-start(f32[576,8,128]{2,1,0:T(8,128)} %shard_map.55.source), channel_id=1, source_target_pairs={{0,128},{16,144},{32,160},{48,176},{64,192},{80,208},{96,224},{112... | collective-permute-start | bytes 7077896 | tf_op jit(solution)/shard_map/ppermute | solution.py:439
  29.8 0.6 pad_add_fusion.1.bounds
  30.4 0.0 copy-done
  30.4 105.6 %shard_map.56.mine = f32[256,4,128]{2,1,0:T(4,128)} custom-call(s32[3]{0:T(128)} %pad_add_fusion.1.bounds, s32[256]{0:T(256)} %bitcast.13, s32[2048]{0:T(1024)} %copy-done, f32[576,8,128]{2,1,0:T(8,128)} %shard_map.55.source), custom_call_target="tpu_custom_call" | custom-call | flops 33554432000 | bytes 4194304 | tf_op jit(solution)/shard_map/pallas_call | solution.py:260
  136.0 0.5 concatenate.9.bounds
  136.5 0.0 collective-permute-done
  136.5 0.5 slice.8.order
  137.0 0.6 slice.9.nbr
  137.6 0.0 collective-permute-done.1.source
  137.6 1.7 %shard_map.57.mine = f32[48,4,128]{2,1,0:T(4,128)} custom-call(s32[3]{0:T(128)} %concatenate.9.bounds, s32[256]{0:T(256)} %slice.8.order, s32[2048]{0:T(1024)} %slice.9.nbr, f32[576,8,128]{2,1,0:T(8,128)} %collective-permute-done.1.source), custom_call_target="tpu_custom_call" | custom-call | flops 6291456000 | bytes 4194304 | tf_op jit(solution)/shard_map/pallas_call | solution.py:260
  139.4 7.8 %shard_map.58.helped = f32[48,4,128]{2,1,0:T(4,128)} custom-call(f32[48,4,128]{2,1,0:T(4,128)} %shard_map.57.mine), custom_call_target="tpu_custom_call" | custom-call | tf_op jit(solution)/shard_map/pallas_call | solution.py:422
  147.2 2.2 %shard_map.59 = f32[256,4,128]{2,1,0:T(4,128)} custom-call(s32[1]{0:T(128)} %bitcast.10.heavy, s32[256]{0:T(256)} %bitcast.14, f32[256,4,128]{2,1,0:T(4,128)} %shard_map.56.mine, f32[48,4,128]{2,1,0:T(4,128)} %shard_map.58.helped), custom_call_target="tpu_custom_call" | custom-call | tf_op jit(solution)/shard_map/pallas_call | solution.py:296
Async XLA Ops:
  0.9 29.5 %copy-start = (s32[2048]{0:T(1024)}, s32[2048]{0:T(1024)S(1)}, u32[]{:S(2)}) copy-start(s32[2048]{0:T(1024)S(1)} %reshape_squeeze.3.nbr) | copy-start | bytes 24580
  25.5 111.0 %collective-permute-start = (s32[2304]{0:T(1024)S(1)}, s32[2304]{0:T(1024)S(1)}, u32[]{:S(2)}, u32[]{:S(2)}) collective-permute-start(s32[2304]{0:T(1024)S(1)} %pad_add_fusion), channel_id=1, source_target_pairs={{0,128},{16,144},{32,160},{48,176},{64,192},{80,208},{96,224},{112... | collective-permute-start | bytes 27656 | tf_op jit(solution)/shard_map/ppermute | solution.py:439
  26.1 111.5 %collective-permute-start.1 = (f32[576,8,128]{2,1,0:T(8,128)}, f32[576,8,128]{2,1,0:T(8,128)}, u32[]{:S(2)}, u32[]{:S(2)}) collective-permute-start(f32[576,8,128]{2,1,0:T(8,128)} %shard_map.55.source), channel_id=1, source_target_pairs={{0,128},{16,144},{32,160},{48,176},{64,192},{80,208},{96,224},{112... | collective-permute-start | bytes 7077896 | tf_op jit(solution)/shard_map/ppermute | solution.py:439

commit v8 on v7

--- a/solution.py
+++ b/solution.py
@@ -14,7 +14,7 @@
 HS_FACE = 64
 HS_CORNER = 16
 EXT = 576
-HELP = 48
+HELP = 52
 OFFSETS = ((-1, -1), (-1, 0), (-1, 1), (0, -1), (0, 1), (1, -1), (1, 0), (1, 1))
 
 SLOPE = -5.0 * 21.0 / (16.0 * math.pi)

time: 150 us -> 148 us (0.987)
  Pallas kernels: 141 us -> 138 us
    pallas_call x2, Pallas kernels: 107 us -> 103 us  [rates_of(): pl.pallas_call(functools.partial(rates_kernel, by_slot=by_slot), out_shap...]
  transfers between devices with their start and end apart: 2 -> 2, of which waited for: 0 -> 0; matrix products, arithmetic and copies ran while one was open for 1% -> 2% of each run, Pallas kernels for 71% -> 69%
where the time goes in v8:
time: 148 us; the launch traced here: 146 us
  Pallas kernels  138 us (93%)
  starting transfers between devices  3.62 us (2%)
  local copies, waits for them, and re-layouts  2.59 us (2%)
    pallas_call x2, Pallas kernels, rates_of(): pl.pallas_call(functools.partial(rates_kernel, by_slot=by_slot), out_shap...  103 us
    pallas_call x1, Pallas kernels, exchange(): pl.pallas_call(kernel, out_shape=jax.ShapeDtypeStruct((starts()[1], 8, 12...  23.9 us
    pallas_call x1, Pallas kernels, swap(): pl.pallas_call(functools.partial(swap_kernel, half), out_shape=jax.ShapeD...  8.77 us
    ppermute x2, starting transfers between devices, shards(): lax.ppermute(v, 'gx', partners)  3.62 us
  transfers between devices with their start and end apart: 2, of which 0 were waited for; matrix products, arithmetic and copies ran while one was open for 2% of the time, Pallas kernels for 69%

profile of v8, /device:TPU:32, one launch (start us, length us, event | category | flops | bytes accessed | tf_op | source)
XLA Modules:
  0.0 146.5 jit_solution(8819517148478773306)
XLA Ops:
  0.0 0.8 copy.6
  0.8 0.1 reshape_squeeze.3.nbr
  0.9 0.0 copy-start
  0.9 0.7 pad_add_fusion
  1.6 23.9 %shard_map.55.source = f32[576,8,128]{2,1,0:T(8,128)} custom-call(s32[64]{0:T(128)} %bitcast.15, f32[256,8,128]{2,1,0:T(8,128)} %bitcast.11), custom_call_target="tpu_custom_call" | custom-call | tf_op jit(solution)/shard_map/pallas_call | solution.py:386
  25.5 0.6 collective-permute-start
  26.1 3.0 %collective-permute-start.1 = (f32[576,8,128]{2,1,0:T(8,128)}, f32[576,8,128]{2,1,0:T(8,128)}, u32[]{:S(2)}, u32[]{:S(2)}) collective-permute-start(f32[576,8,128]{2,1,0:T(8,128)} %shard_map.55.source), channel_id=1, source_target_pairs={{0,128},{16,144},{32,160},{48,176},{64,192},{80,208},{96,224},{112... | collective-permute-start | bytes 7077896 | tf_op jit(solution)/shard_map/ppermute | solution.py:439
  29.8 0.6 pad_add_fusion.1.bounds
  30.4 0.0 copy-done
  30.4 101.7 %shard_map.56.mine = f32[256,4,128]{2,1,0:T(4,128)} custom-call(s32[3]{0:T(128)} %pad_add_fusion.1.bounds, s32[256]{0:T(256)} %bitcast.13, s32[2048]{0:T(1024)} %copy-done, f32[576,8,128]{2,1,0:T(8,128)} %shard_map.55.source), custom_call_target="tpu_custom_call" | custom-call | flops 33554432000 | bytes 4194304 | tf_op jit(solution)/shard_map/pallas_call | solution.py:260
  132.1 0.5 concatenate.9.bounds
  132.6 0.0 collective-permute-done
  132.6 0.5 slice.8.order
  133.2 0.6 slice.9.nbr
  133.8 0.0 collective-permute-done.1.source
  133.8 1.7 %shard_map.57.mine = f32[52,4,128]{2,1,0:T(4,128)} custom-call(s32[3]{0:T(128)} %concatenate.9.bounds, s32[256]{0:T(256)} %slice.8.order, s32[2048]{0:T(1024)} %slice.9.nbr, f32[576,8,128]{2,1,0:T(8,128)} %collective-permute-done.1.source), custom_call_target="tpu_custom_call" | custom-call | flops 6815744000 | bytes 4194304 | tf_op jit(solution)/shard_map/pallas_call | solution.py:260
  135.5 8.8 %shard_map.58.helped = f32[52,4,128]{2,1,0:T(4,128)} custom-call(f32[52,4,128]{2,1,0:T(4,128)} %shard_map.57.mine), custom_call_target="tpu_custom_call" | custom-call | tf_op jit(solution)/shard_map/pallas_call | solution.py:422
  144.3 2.2 %shard_map.59 = f32[256,4,128]{2,1,0:T(4,128)} custom-call(s32[1]{0:T(128)} %bitcast.10.heavy, s32[256]{0:T(256)} %bitcast.14, f32[256,4,128]{2,1,0:T(4,128)} %shard_map.56.mine, f32[52,4,128]{2,1,0:T(4,128)} %shard_map.58.helped), custom_call_target="tpu_custom_call" | custom-call | tf_op jit(solution)/shard_map/pallas_call | solution.py:296
Async XLA Ops:
  0.9 29.5 %copy-start = (s32[2048]{0:T(1024)}, s32[2048]{0:T(1024)S(1)}, u32[]{:S(2)}) copy-start(s32[2048]{0:T(1024)S(1)} %reshape_squeeze.3.nbr) | copy-start | bytes 24580
  25.5 107.1 %collective-permute-start = (s32[2304]{0:T(1024)S(1)}, s32[2304]{0:T(1024)S(1)}, u32[]{:S(2)}, u32[]{:S(2)}) collective-permute-start(s32[2304]{0:T(1024)S(1)} %pad_add_fusion), channel_id=1, source_target_pairs={{0,128},{16,144},{32,160},{48,176},{64,192},{80,208},{96,224},{112... | collective-permute-start | bytes 27656 | tf_op jit(solution)/shard_map/ppermute | solution.py:439
  26.1 107.6 %collective-permute-start.1 = (f32[576,8,128]{2,1,0:T(8,128)}, f32[576,8,128]{2,1,0:T(8,128)}, u32[]{:S(2)}, u32[]{:S(2)}) collective-permute-start(f32[576,8,128]{2,1,0:T(8,128)} %shard_map.55.source), channel_id=1, source_target_pairs={{0,128},{16,144},{32,160},{48,176},{64,192},{80,208},{96,224},{112... | collective-permute-start | bytes 7077896 | tf_op jit(solution)/shard_map/ppermute | solution.py:439
